TPU v7x, 32 devices: a whole 2x2x4 slice. The times are simulated.
32 devices in a mesh: alpha: 8 (over z, core), beta: 4 (over y, x).
Axes of the slice: x: 2, y: 2, z: 4, core: 2. Of those that a mesh axis runs over, the one named last changes fastest.
Arguments:
- coefficients: bfloat16 [4096, 4096], P('alpha', 'beta'), may hold values from -6 to 6
- diagonal: float32 [4096, 4096], P('alpha', 'beta'), may hold values from 0.5 to 2
- alpha_blocks: bfloat16 [32, 14, 128, 128], P('alpha'), may hold values from -0.125 to 0.125
- alpha_lists: int32 [32, 14], replicated, may hold values from 0 to 31, as said below
- beta_blocks: bfloat16 [32, 14, 128, 128], P('beta'), may hold values from -0.125 to 0.125
- beta_lists: int32 [32, 14], replicated, may hold values from 0 to 31, as said below
Outputs:
- sigma_out: bfloat16 [4096, 4096], P('alpha', 'beta')
Inputs may be any that keep to these rules, and one draw needn't show every extreme that they name: `alpha_lists`: each row names 14 different blocks. For every alpha device, the rows of its 4 block rows name at most 2 different blocks owned by any one alpha device (blocks j * 4 to (j + 1) * 4 - 1 belong to device j), and exactly 2 from some owner. `beta_lists`: each row names 14 different blocks. For every beta device, the rows of its 8 block rows name at most 4 different blocks owned by any one beta device (blocks j * 8 to (j + 1) * 8 - 1 belong to device j), and exactly 4 from some owner.
All inputs are finite; a program needn't handle non-finite values.
Results may differ from a plain program's by a relative error of at most 0.001.
Values may be sent and summed in bfloat16 or wider, within the bound.
No kernel may reach another device: no remote copies, remote signals or barrier semaphores. Data moves between devices by JAX's collectives and lax.ppermute only.
A program may use at most 128 MiB of HBM per device.

v0:
```python
import jax
import jax.numpy as jnp
from jax import lax
from jax.sharding import PartitionSpec as P

CAP_B = 4


def piece_weights(list_ids, number, blocks_here):
    hits = (list_ids[:, :, None] == jnp.arange(number, dtype=jnp.int32)).astype(jnp.bfloat16)
    combined = jnp.einsum("rkj,rkab->rjab", hits, blocks_here, preferred_element_type=jnp.float32)
    return combined.astype(jnp.bfloat16)


def wanted(columns, first_id, number):
    targets = first_id + jnp.arange(number, dtype=jnp.int32)
    return jnp.any(columns[..., :, None] == targets, axis=-2)


def slot_onehot(needed, limit):
    position = jnp.cumsum(needed.astype(jnp.int32), axis=-1) - 1
    hits = needed[..., None] & (position[..., None] == jnp.arange(limit, dtype=jnp.int32))
    return hits.astype(jnp.bfloat16)


def slot_index(list_ids, owners, per_owner, limit):
    needed = wanted(list_ids.reshape(1, -1), 0, owners * per_owner)[0]
    position = jnp.cumsum(needed.reshape(owners, per_owner).astype(jnp.int32), axis=-1) - 1
    return list_ids // per_owner * limit + jnp.take(position.reshape(-1), list_ids)


def per_device(coefficients, diagonal, alpha_blocks, alpha_lists, beta_blocks, beta_lists):
    block = alpha_blocks.shape[2]
    rows_a = alpha_blocks.shape[0]
    rows_b = beta_blocks.shape[0]
    height = coefficients.shape[0]
    columns_dev = coefficients.shape[1]
    owners_b = lax.axis_size("beta")
    index_a = lax.axis_index("alpha")
    index_b = lax.axis_index("beta")
    mine_a = lax.dynamic_slice_in_dim(alpha_lists, index_a * rows_a, rows_a, 0)
    mine_b = lax.dynamic_slice_in_dim(beta_lists, index_b * rows_b, rows_b, 0)
    piece_rows = lax.all_gather(coefficients, "alpha", axis=0, tiled=True)
    number = piece_rows.shape[0] // block
    combined = piece_weights(mine_a, number, alpha_blocks)
    piece_blocks = piece_rows.reshape(number, block, columns_dev)
    alpha_term = jnp.einsum(
        "rjab,jbn->ran", combined, piece_blocks, preferred_element_type=jnp.float32
    ).reshape(height, columns_dev)
    needed_b = wanted(
        beta_lists.reshape(owners_b, rows_b * beta_blocks.shape[1]), index_b * rows_b, rows_b
    )
    onehot_b = slot_onehot(needed_b, CAP_B)
    outgoing_b = jnp.einsum(
        "djc,mjb->dcmb",
        onehot_b,
        coefficients.reshape(height, rows_b, block),
        preferred_element_type=jnp.float32,
    ).astype(jnp.bfloat16)
    arrived_b = lax.all_to_all(outgoing_b, "beta", split_axis=0, concat_axis=0, tiled=True)
    slot_ids_b = slot_index(mine_b, owners_b, rows_b, CAP_B)
    chosen_b = jnp.take(arrived_b.reshape(owners_b * CAP_B, height, block), slot_ids_b, axis=0)
    beta_term = jnp.einsum(
        "rkmb,rkab->mra", chosen_b, beta_blocks, preferred_element_type=jnp.float32
    ).reshape(height, columns_dev)
    sigma_out = alpha_term + beta_term + diagonal * coefficients.astype(jnp.float32)
    return sigma_out.astype(jnp.bfloat16)


def solution(mesh):
    in_specs = (
        P("alpha", "beta"),
        P("alpha", "beta"),
        P("alpha", None, None, None),
        P(),
        P("beta", None, None, None),
        P(),
    )
    out_specs = P("alpha", "beta")
    return jax.shard_map(
        per_device, mesh=mesh, in_specs=in_specs, out_specs=out_specs, check_vma=False
    )
```

profile of v0, /device:TPU:0, one launch (start us, length us, event | category | flops | bytes accessed | tf_op | source)
XLA Modules:
  0.0 110.6 jit_solution(11732586952250578745)
XLA Ops:
  6.5 0.7 all-gather.2.cloned.1.call-update
  7.3 0.8 copy.22
  8.0 0.1 eq.71
  8.1 0.2 compare_reduce_fusion
  8.4 1.5 %copy.30 = bf16[64,8,8,128]{3,2,1,0:T(8,128)(2,1)S(1)} copy(bf16[64,8,8,128]{3,1,2,0:T(8,128)(2,1)} %bitcast.39) | data formatting | bytes 2097152
  9.9 0.2 reduce_window_sum.18
  10.0 2.0 %convolution_convert_fusion.1 = bf16[4,4,512,128]{3,1,2,0:T(4,128)(2,1)} fusion(bf16[512,8,128,1]{2,1,0,3:T(8,128)(2,1)S(1)} %bitcast.37, s32[4,8]{1,0:T(4,128)S(1)} %broadcast_add_fusion, pred[4,8]{1,0:T(4,128)(4,1)S(1)} %compare_reduce_fusion), kind=kOutput, calls=%fused_computation.13 | convolution fusion | flops 17826048 | bytes 3145888 | tf_op jit(solution)/shard_map/djc,mjb->dcmb/dot_general | solution.py:54
  12.1 5.3 %all-to-all-start = ((bf16[4,4,512,128]{3,1,2,0:T(4,128)(2,1)}), bf16[4,4,512,128]{3,1,2,0:T(4,128)(2,1)}, u32[]{:S(2)}, u32[]{:S(2)}) async-start(bf16[4,4,512,128]{3,1,2,0:T(4,128)(2,1)} %convolution_convert_fusion.1), calls=%async_computation | async-start | bytes 4194304 | tf_op jit(solution)/shard_map/all_to_all | solution.py:60
  17.4 0.1 eq.67
  17.4 0.1 fusion.14
  17.6 0.1 reshape.91
  17.6 0.2 reduce_window_sum.17
  17.8 0.1 sub.16
  18.0 1.2 %gather_fusion = s32[112]{0:T(128)S(1)} fusion(s32[32]{0:T(128)S(1)} %sub.16, s32[1024]{0:T(1024)S(1)} %pad_clamp_fusion.1), kind=kCustom, calls=%fused_computation | custom fusion | bytes 1344 | tf_op jit(solution)/shard_map/jit(_take)/gather | solution.py:29
  19.4 0.1 reshape.102
  19.5 0.1 copy.19
  19.6 3.8 %convolution_convert_fusion = bf16[4,32,128,128]{3,1,2,0:T(8,128)(2,1)} fusion(bf16[4,14,128,128]{3,2,1,0:T(8,128)(2,1)S(1)} %copy-done, s32[4,14]{1,0:T(4,128)S(1)} %copy.19), kind=kOutput, calls=%fused_computation.8 | convolution fusion | flops 60819200 | bytes 6029536 | tf_op jit(solution)/shard_map/rkj,rkab->rjab/dot_general | solution.py:11
  23.4 19.7 %all-to-all-done = bf16[4,4,512,128]{3,1,2,0:T(4,128)(2,1)} async-done(((bf16[4,4,512,128]{3,1,2,0:T(4,128)(2,1)}), bf16[4,4,512,128]{3,1,2,0:T(4,128)(2,1)}, u32[]{:S(2)}, u32[]{:S(2)}) %all-to-all-start) | async-done | bytes 2097184 | tf_op jit(solution)/shard_map/all_to_all | solution.py:60
  43.1 3.4 %copy.24 = bf16[4,4,512,128]{3,2,1,0:T(8,128)(2,1)} copy(bf16[4,4,512,128]{3,1,2,0:T(4,128)(2,1)} %all-to-all-done) | data formatting | bytes 4194304 | tf_op jit(solution)/shard_map/all_to_all | solution.py:60
  46.4 9.3 %gather_fusion.1 = bf16[112,512,128]{2,1,0:T(8,128)(2,1)} fusion(bf16[16,512,128]{2,1,0:T(8,128)(2,1)} %bitcast.35, s32[1024]{0:T(1024)S(1)} %pad_clamp_fusion), kind=kCustom, calls=%fused_computation.1 | custom fusion | bytes 29360576 | tf_op jit(solution)/shard_map/jit(_take)/gather | solution.py:62
  55.8 10.3 %fusion = f32[8,512,128,1]{1,2,3,0:T(8,128)} fusion(bf16[8,14,128,128]{3,2,1,0:T(8,128)(2,1)} %param.10, bf16[8,14,512,128]{3,2,1,0:T(8,128)(2,1)} %bitcast.36, pred[8,14]{1,0:T(8,128)(4,1)S(1)} %get-tuple-element.5), kind=kOutput, calls=%fused_computation.2 | convolution fusion | flops 1886388224 | bytes 20447344 | tf_op jit(solution)/shard_map/rkmb,rkab->mra/dot_general | solution.py:63
  66.1 3.0 %copy.29 = f32[512,1024]{1,0:T(8,128)} copy(f32[512,1024]{0,1:T(8,128)} %bitcast.40) | data formatting | bytes 4194304 | tf_op jit(solution)/shard_map/reshape | solution.py:65
  69.2 24.6 %all-gather.2.cloned.1.call-done = bf16[4096,1024]{1,0:T(8,128)(2,1)} async-done(((bf16[512,1024]{1,0:T(8,128)(2,1)}), bf16[4096,1024]{1,0:T(8,128)(2,1)}) %all-gather.2.cloned.1.call-update) | async-done | bytes 8388624 | tf_op jit(solution)/shard_map/all_gather | solution.py:43
  93.8 10.0 %fusion.7 = bf16[512,1024]{1,0:T(8,128)(2,1)} fusion(f32[512,1024]{1,0:T(8,128)} %copy.29, f32[512,1024]{1,0:T(8,128)} %param.7, bf16[512,1024]{1,0:T(8,128)(2,1)S(1)} %copy-done.1, bf16[32,128,1024]{2,1,0:T(8,128)(2,1)} %bitcast.41, bf16[512,128,32]{1,2,0:T(8,128)(2,1)} %bitcast.38), kind=kOutput, calls=%fused_computation.11 | convolution fusion | flops 4297588736 | bytes 18874368 | tf_op jit(solution)/shard_map/rjab,jbn->ran/dot_general | solution.py:47
  (19 shorter events, 0.3 us)
Async XLA Ops:
  6.5 13.1 %copy-start = (bf16[4,14,128,128]{3,2,1,0:T(8,128)(2,1)S(1)}, bf16[4,14,128,128]{3,2,1,0:T(8,128)(2,1)}, u32[]{:S(2)}) copy-start(bf16[4,14,128,128]{3,2,1,0:T(8,128)(2,1)} %param.8) | copy-start | bytes 5505028
  6.5 87.2 %all-gather.2.cloned.1.call-start = ((), (), s32[]{:S(2)}) async-start(), calls=%async_computation.1 | async-start | bytes 9437184 | tf_op jit(solution)/shard_map/all_gather | solution.py:43
  12.1 7.4 %copy-start.2 = (s32[32,14]{0,1:T(8,128)S(1)}, s32[32,14]{0,1:T(8,128)}, u32[]{:S(2)}) copy-start(s32[32,14]{0,1:T(8,128)} %param.9) | copy-start | bytes 5380
  12.1 31.0 %all-to-all-start = ((bf16[4,4,512,128]{3,1,2,0:T(4,128)(2,1)}), bf16[4,4,512,128]{3,1,2,0:T(4,128)(2,1)}, u32[]{:S(2)}, u32[]{:S(2)}) async-start(bf16[4,4,512,128]{3,1,2,0:T(4,128)(2,1)} %convolution_convert_fusion.1), calls=%async_computation | async-start | bytes 4194304 | tf_op jit(solution)/shard_map/all_to_all | solution.py:60
  66.1 27.6 %copy-start.1 = (bf16[512,1024]{1,0:T(8,128)(2,1)S(1)}, bf16[512,1024]{1,0:T(8,128)(2,1)}, u32[]{:S(2)}) copy-start(bf16[512,1024]{1,0:T(8,128)(2,1)} %param.6) | copy-start | bytes 3145732
Sparse Core Ops, SparseCore 0:
  9.0 84.7 all-gather.1
where the time goes:
time: 111 us
  waiting for transfers between devices  45 us (41%)
  matrix products  26.1 us (24%)
  local copies, waits for them, and re-layouts  20 us (18%)
  between operations  13.5 us (12%)
  starting transfers between devices  5.3 us (5%)
    all_gather x1, waiting for transfers between devices, per_device(): piece_rows = lax.all_gather(coefficients, 'alpha', axis=0, tiled=True)  24.6 us
    all_to_all x1, waiting for transfers between devices, per_device(): lax.all_to_all(outgoing_b, 'beta', split_axis=0, concat_axis=0, tiled=True)  19.7 us
    dot_general x1, matrix products, per_device(): jnp.einsum('rkmb,rkab->mra', chosen_b, beta_blocks, preferred_element_typ...  10.3 us
    dot_general x1, matrix products, per_device(): jnp.einsum('rjab,jbn->ran', combined, piece_blocks, preferred_element_typ...  9.95 us
    gather x1, local copies, waits for them, and re-layouts, per_device(): jnp.take(arrived_b.reshape(owners_b * CAP_B, height, block), slot_ids_b,...  9.33 us
    all_to_all x1, starting transfers between devices, per_device(): lax.all_to_all(outgoing_b, 'beta', split_axis=0, concat_axis=0, tiled=True)  5.29 us
    dot_general x1, matrix products, piece_weights(): jnp.einsum('rkj,rkab->rjab', hits, blocks_here, preferred_element_type=jn...  3.76 us
    all_to_all x1, local copies, waits for them, and re-layouts, per_device(): lax.all_to_all(outgoing_b, 'beta', split_axis=0, concat_axis=0, tiled=True)  3.36 us
  transfers between devices with their start and end apart: 2, of which 2 were waited for; matrix products, arithmetic and copies ran while one was open for 33% of the time, Pallas kernels for 0%

commit v1 on v0

v1 whole, which is shorter than its diff:
```python
import functools

import jax
import jax.numpy as jnp
import numpy as np
from jax import lax
from jax.experimental import pallas as pl
from jax.experimental.pallas import tpu as pltpu
from jax.sharding import PartitionSpec as P

CAP_B = 4
CORES = 2
STEP = 1
VMEM_LIMIT = 40 * 1024 * 1024


def beta_tables(beta_lists, me, owners, per_owner):
    number = owners * per_owner
    ids = jnp.arange(number, dtype=jnp.int32)
    flat = beta_lists.reshape(owners, -1)
    needed = jnp.any(flat[:, :, None] == ids, axis=1)
    same = (ids[:, None] // per_owner == ids[None, :] // per_owner) & (ids[:, None] < ids[None, :])
    rank = jnp.sum((needed[:, :, None] & same).astype(jnp.int32), axis=1)
    caps = jnp.arange(CAP_B, dtype=jnp.int32)
    match = needed[:, :, None] & (rank[:, :, None] == caps)
    match = match.reshape(owners, owners, per_owner, CAP_B)
    local = jnp.arange(per_owner, dtype=jnp.int32)[:, None]
    chosen = jnp.max(jnp.where(match, local, -1), axis=2)
    steps = np.arange(1, owners)
    pack = lax.dynamic_index_in_dim(chosen, me, 1, keepdims=False)
    pack = jnp.take(pack, partner(me, steps, owners), axis=0)
    got = lax.dynamic_index_in_dim(chosen, me, 0, keepdims=False)
    got = jnp.where(got >= 0, got + jnp.arange(owners, dtype=jnp.int32)[:, None] * per_owner, -1)
    got = jnp.take(got, partner_back(me, steps, owners), axis=0).reshape(-1)
    got = jnp.concatenate([me * per_owner + jnp.arange(per_owner, dtype=jnp.int32), got])
    return jnp.maximum(pack, 0).reshape(-1), got


def partner(me, step, owners):
    if owners & (owners - 1) == 0:
        return me ^ step
    return (me + step) % owners


def partner_back(me, step, owners):
    if owners & (owners - 1) == 0:
        return me ^ step
    return (me + owners - step) % owners


def slot_table(lists, position_ids):
    slots = jnp.arange(lists.shape[1], dtype=jnp.int32)[None, :, None]
    hit = lists[:, :, None] == position_ids[None, None, :]
    return jnp.max(jnp.where(hit, slots, -1), axis=1)


def pack_beta_body(block, pack_ref, c_ref, *outs):
    for s, out in enumerate(outs):
        for c in range(CAP_B):
            j = pack_ref[s * CAP_B + c]
            column = pl.ds(pl.multiple_of(j * block, block), block)
            out[:, c * block : (c + 1) * block] = c_ref[:, column]


def pack_beta(pack, coefficients, parts, block):
    height = coefficients.shape[0]
    shape = jax.ShapeDtypeStruct((height, CAP_B * block), coefficients.dtype)
    return pl.pallas_call(
        functools.partial(pack_beta_body, block),
        grid_spec=pltpu.PrefetchScalarGridSpec(
            num_scalar_prefetch=1,
            grid=(),
            in_specs=[pl.BlockSpec(memory_space=pltpu.VMEM)],
            out_specs=[pl.BlockSpec(memory_space=pltpu.VMEM)] * parts,
        ),
        out_shape=[shape] * parts,
        compiler_params=pltpu.CompilerParams(vmem_limit_bytes=VMEM_LIMIT),
        name="pack_beta",
    )(pack, coefficients)


def fill(weights, table_ref, h_ref, rows, positions, block, first=0):
    for i in range(first, first + rows):
        for q in range(positions):
            k = table_ref[i * positions + q]
            tile = h_ref[i - first, jnp.maximum(k, 0)]
            weights[i * block : (i + 1) * block, q * block : (q + 1) * block] = jnp.where(
                k >= 0, tile, jnp.zeros_like(tile)
            )


def beta_body(rows, positions, block, table_ref, h_ref, d_ref, c_ref, *rest):
    arrived, out_ref, weights = rest[:-2], rest[-2], rest[-1]
    fill(weights, table_ref, h_ref, rows, positions, block)
    own = c_ref[...]
    x = jnp.concatenate([own] + [a[...] for a in arrived], axis=1)
    total = lax.dot_general(
        x, weights[...], (((1,), (1,)), ((), ())), preferred_element_type=jnp.float32
    )
    out_ref[...] = total + d_ref[...] * own.astype(jnp.float32)


def beta_product(table, beta_blocks, coefficients, diagonal, arrived):
    rows, block = beta_blocks.shape[0], beta_blocks.shape[2]
    positions = table.shape[1]
    return pl.pallas_call(
        functools.partial(beta_body, rows, positions, block),
        grid_spec=pltpu.PrefetchScalarGridSpec(
            num_scalar_prefetch=1,
            grid=(),
            in_specs=[pl.BlockSpec(memory_space=pltpu.VMEM)] * (3 + len(arrived)),
            out_specs=pl.BlockSpec(memory_space=pltpu.VMEM),
            scratch_shapes=[pltpu.VMEM((rows * block, positions * block), jnp.bfloat16)],
        ),
        out_shape=jax.ShapeDtypeStruct(diagonal.shape, jnp.float32),
        compiler_params=pltpu.CompilerParams(vmem_limit_bytes=VMEM_LIMIT),
        name="beta_product",
    )(table.reshape(-1), beta_blocks, diagonal, coefficients, *arrived)


def alpha_body(rows, positions, block, table_ref, h_refs, add_refs, piece_refs, out_refs, weights):
    for n, h_ref in enumerate(h_refs):
        fill(weights, table_ref, h_ref, rows, positions, block, n * rows)
    x = jnp.concatenate([p[...] for p in piece_refs], axis=0)
    height = rows * block
    for n, out_ref in enumerate(out_refs):
        total = jnp.dot(weights[n * height : (n + 1) * height], x, preferred_element_type=jnp.float32)
        if add_refs:
            total = total + add_refs[n][...]
        out_ref[...] = total.astype(out_ref.dtype)


def alpha_product(table, blocks, adds, pieces, dtype):
    rows, block = blocks[0].shape[0], blocks[0].shape[2]
    positions = table.shape[1]
    height, width = rows * block, pieces[0].shape[1]

    def body(table_ref, *rest):
        h_refs, rest = rest[: len(blocks)], rest[len(blocks) :]
        add_refs, rest = rest[: len(adds)], rest[len(adds) :]
        piece_refs, rest = rest[: len(pieces)], rest[len(pieces) :]
        alpha_body(rows, positions, block, table_ref, h_refs, add_refs, piece_refs, rest[:-1], rest[-1])

    return pl.pallas_call(
        body,
        grid_spec=pltpu.PrefetchScalarGridSpec(
            num_scalar_prefetch=1,
            grid=(),
            in_specs=[pl.BlockSpec(memory_space=pltpu.VMEM)] * (len(blocks) + len(adds) + len(pieces)),
            out_specs=[pl.BlockSpec(memory_space=pltpu.VMEM)] * len(blocks),
            scratch_shapes=[pltpu.VMEM((len(blocks) * height, positions * block), jnp.bfloat16)],
        ),
        out_shape=[jax.ShapeDtypeStruct((height, width), dtype)] * len(blocks),
        compiler_params=pltpu.CompilerParams(vmem_limit_bytes=VMEM_LIMIT),
        name="alpha_product",
    )(table.reshape(-1), *blocks, *adds, *pieces)


def send(x, edges):
    return lax.ppermute(x, "alpha", [(s * CORES + c, t * CORES + c) for s, t in edges for c in range(CORES)])


def swap(x, chips):
    return lax.ppermute(x, "alpha", [(p * CORES + c, p * CORES + 1 - c) for p in chips for c in range(CORES)])


def gate(*values):
    return lax.optimization_barrier(values)


def block_ids(places, rows):
    ids = np.full((len(places), CORES, len(places[0])), -1, np.int32)
    for p, line in enumerate(places):
        for g, place in enumerate(line):
            if place is not None:
                for c in range(CORES):
                    ids[p, c, g] = (place[0] * CORES + c) * rows + place[1]
    return ids


def per_device(coefficients, diagonal, alpha_blocks, alpha_lists, beta_blocks, beta_lists):
    block = alpha_blocks.shape[2]
    rows_a, rows_b = alpha_blocks.shape[0], beta_blocks.shape[0]
    chips = lax.axis_size("alpha") // CORES
    owners_b = lax.axis_size("beta")
    index_a, index_b = lax.axis_index("alpha"), lax.axis_index("beta")
    core = lax.rem(index_a, CORES)
    height = rows_a * block
    span = STEP * block
    cuts = rows_a // STEP

    pack, beta_ids = beta_tables(beta_lists, index_b, owners_b, rows_b)
    mine_b = lax.dynamic_slice_in_dim(beta_lists, index_b * rows_b, rows_b, 0)

    def place(chip, first, count):
        return [(chip, first + g) if 0 <= chip < chips else None for g in range(count)]

    def table_of(places, lists, swapped):
        ids = [block_ids(p, rows_a) for p in places]
        if swapped:
            ids = ids + [i[:, ::-1] for i in ids]
        ids = jnp.asarray(np.concatenate(ids, axis=2).reshape(chips * CORES, -1))
        return slot_table(lists, lax.dynamic_index_in_dim(ids, index_a, 0, keepdims=False))

    mine_a = lax.dynamic_slice_in_dim(alpha_lists, index_a * rows_a, rows_a, 0)
    theirs_a = lax.dynamic_slice_in_dim(alpha_lists, (index_a + 1 - 2 * core) * rows_a, rows_a, 0)
    both = jnp.concatenate([mine_a, theirs_a], axis=0)
    table_b = slot_table(mine_b, beta_ids)

    def beta_all(arrived):
        return beta_product(table_b, beta_blocks, coefficients, diagonal, arrived)

    def exchange(packed):
        steps = range(1, owners_b)
        return [
            lax.ppermute(packed[s - 1], "beta", [(d, partner(d, s, owners_b)) for d in range(owners_b)]) for s in steps
        ]

    def product(table, pieces, adds):
        return alpha_product(table, [alpha_blocks, other_blocks], adds, pieces, jnp.float32)

    def last_product(table, pieces, acc):
        return alpha_product(table, [alpha_blocks], [acc], pieces, jnp.bfloat16)[0]

    everyone = range(chips)
    own = [place(p, 0, rows_a) for p in everyone]
    if chips == 4:
        far, near = [(0, 2), (1, 3), (2, 0), (3, 1)], [(0, 1), (1, 0), (2, 3), (3, 2)]
        far_from, near_from, both_from = [2, 3, 0, 1], [1, 0, 3, 2], [3, 2, 1, 0]

        def of(chip_of):
            return [place(chip_of[p], 0, rows_a) for p in everyone]

        table_here = table_of([own, of(near_from), of(far_from)], mine_a, True)
        table_both = table_of([of(both_from)], mine_a, True)

        near_own, far_own = send(coefficients, near), send(coefficients, far)
        arrived = exchange(pack_beta(pack, coefficients, owners_b - 1, block))
        near_own, far_own, here, table_here, table_both, table_b, *arrived = gate(
            near_own, far_own, coefficients, table_here, table_both, table_b, *arrived
        )

        near_far = send(far_own, near)
        pieces = [here, near_own, far_own]
        pieces += [swap(x, everyone) for x in pieces]
        *pieces, here = gate(*pieces, here)
        acc = beta_product(table_b, beta_blocks, here, diagonal, arrived)
        (acc,) = alpha_product(table_here, [alpha_blocks], [acc], pieces, jnp.float32)
        near_far, acc = gate(near_far, acc)
        return last_product(table_both, [near_far, swap(near_far, everyone)], acc)

    other_blocks = swap(alpha_blocks, everyone)
    arrived = exchange(pack_beta(pack, coefficients, owners_b - 1, block))
    pieces, places = [coefficients], [own]
    left, right = [], []
    for u in range((chips - 1) * cuts):
        kind, v = u // cuts, u % cuts
        mine = coefficients[v * span : (v + 1) * span]
        left.append(send(mine if u < cuts else left[u - cuts], [(p, p - 1) for p in range(1, chips) if kind < chips - p]))
        right.append(send(mine if u < cuts else right[u - cuts], [(p, p + 1) for p in range(chips - 1) if kind < p + 1]))
        pieces += [left[u], right[u]]
        places += [
            [place(p + 1 + kind, v * STEP, STEP) for p in everyone],
            [place(p - 1 - kind, v * STEP, STEP) for p in everyone],
        ]
    sums = []
    for k in range(0, len(pieces) - 2, 4):
        upto = min(k + 4, len(pieces) - 2)
        sums = product(table_of(places[k:upto], both, False), pieces[k:upto], sums)
    acc = beta_all(arrived) + sums[0] + swap(sums[1], everyone)
    ends = pieces[-2:]
    return last_product(table_of(places[-2:], mine_a, True), ends + [swap(x, everyone) for x in ends], acc)


def solution(mesh):
    in_specs = (
        P("alpha", "beta"),
        P("alpha", "beta"),
        P("alpha", None, None, None),
        P(),
        P("beta", None, None, None),
        P(),
    )
    out_specs = P("alpha", "beta")
    return jax.shard_map(
        per_device, mesh=mesh, in_specs=in_specs, out_specs=out_specs, check_vma=False
    )
```

time: 111 us -> 86.3 us (0.78)
  matrix products: 26.1 us -> 0 us
  Pallas kernels: 0 us -> 16.8 us
  between operations: 13.5 us -> 0.11 us
  waiting for transfers between devices: 45 us -> 37.6 us
  starting transfers between devices: 5.3 us -> 11.1 us
  local copies, waits for them, and re-layouts: 20 us -> 18.2 us
  other arithmetic: 0.76 us -> 1.99 us
    ppermute x0 -> x10, waiting for transfers between devices: none -> 37.6 us  [the longest x3 18.6 us: exchange(): lax.ppermute(packed[s - 1], 'beta', [(d, partner(d, s, owners_b)) for d i...]
    dot_general x4 -> x0, matrix products: 26.1 us -> none  [the longest x1 10.3 us: per_device(): jnp.einsum('rkmb,rkab->mra', chosen_b, beta_blocks, preferred_element_typ...]
    all_gather x1 -> x0, waiting for transfers between devices: 24.6 us -> none  [per_device(): piece_rows = lax.all_gather(coefficients, 'alpha', axis=0, tiled=True)]
    all_to_all x1 -> x0, waiting for transfers between devices: 19.7 us -> none  [per_device(): lax.all_to_all(outgoing_b, 'beta', split_axis=0, concat_axis=0, tiled=True)]
    pallas_call x0 -> x4, Pallas kernels: none -> 16.8 us  [the longest x2 9.66 us: alpha_product(): pl.pallas_call(body, grid_spec=pltpu.PrefetchScalarGridSpec(num_scalar_pr...]
    unnamed x8 -> x33, local copies, waits for them, and re-layouts: 2.28 us -> 14.1 us
    ppermute x0 -> x10, starting transfers between devices: none -> 11.1 us  [the longest x3 7.1 us: send(): lax.ppermute(x, 'alpha', [(s * CORES + c, t * CORES + c) for s, t in edge...]
    gather x3 -> x2, local copies, waits for them, and re-layouts: 10.6 us -> 1.11 us  [the longest x1 0.56 us: beta_tables(): got = jnp.take(got, partner_back(me, steps, owners), axis=0).reshape(-1)]
  transfers between devices with their start and end apart: 2 -> 10, of which waited for: 2 -> 8; matrix products, arithmetic and copies ran while one was open for 33% -> 8% of each run, Pallas kernels for 0% -> 15%
where the time goes in v1:
time: 86.3 us; the launch traced here: 85.7 us
  waiting for transfers between devices  37.6 us (44%)
  local copies, waits for them, and re-layouts  18.2 us (21%)
  Pallas kernels  16.8 us (19%)
  starting transfers between devices  11.1 us (13%)
  other arithmetic  1.99 us (2%)
    ppermute x3, waiting for transfers between devices, exchange(): lax.ppermute(packed[s - 1], 'beta', [(d, partner(d, s, owners_b)) for d i...  18.6 us
    ppermute x3, waiting for transfers between devices, send(): lax.ppermute(x, 'alpha', [(s * CORES + c, t * CORES + c) for s, t in edge...  14.5 us
    unnamed x33, local copies, waits for them, and re-layouts  14.1 us
    pallas_call x2, Pallas kernels, alpha_product(): pl.pallas_call(body, grid_spec=pltpu.PrefetchScalarGridSpec(num_scalar_pr...  9.66 us
    ppermute x3, starting transfers between devices, send(): lax.ppermute(x, 'alpha', [(s * CORES + c, t * CORES + c) for s, t in edge...  7.1 us
    pallas_call x1, Pallas kernels, beta_product(): pl.pallas_call(functools.partial(beta_body, rows, positions, block), grid...  5.08 us
    ppermute x4, waiting for transfers between devices, swap(): lax.ppermute(x, 'alpha', [(p * CORES + c, p * CORES + 1 - c) for p in chi...  4.43 us
    ppermute x3, starting transfers between devices, exchange(): lax.ppermute(packed[s - 1], 'beta', [(d, partner(d, s, owners_b)) for d i...  3.49 us
  transfers between devices with their start and end apart: 10, of which 8 were waited for; matrix products, arithmetic and copies ran while one was open for 8% of the time, Pallas kernels for 15%

profile of v1, /device:TPU:0, one launch (start us, length us, event | category | flops | bytes accessed | tf_op | source)
XLA Modules:
  0.0 85.7 jit_solution(17156259588461540010)
XLA Ops:
  0.0 4.0 %collective-permute-start.1 = (bf16[512,1024]{1,0:T(8,128)(2,1)}, bf16[512,1024]{1,0:T(8,128)(2,1)S(1)}, u32[]{:S(2)}, u32[]{:S(2)}) collective-permute-start(bf16[512,1024]{1,0:T(8,128)(2,1)} %rest_2_), channel_id=1, source_target_pairs={{0,16},{4,20},{8,24},{12,28},{16,0},{20,4},{24,8},{28,12},{1,17},{... | collective-permute-start | bytes 3145736 | tf_op jit(solution)/shard_map/ppermute | solution.py:160
  4.0 1.6 %collective-permute-start = (bf16[512,1024]{1,0:T(8,128)(2,1)}, bf16[512,1024]{1,0:T(8,128)(2,1)S(1)}, u32[]{:S(2)}, u32[]{:S(2)}) collective-permute-start(bf16[512,1024]{1,0:T(8,128)(2,1)} %rest_2_), channel_id=1, source_target_pairs={{0,8},{4,12},{8,0},{12,4},{16,24},{20,28},{24,16},{28,20},{1,9},{5... | collective-permute-start | bytes 3145736 | tf_op jit(solution)/shard_map/ppermute | solution.py:160
  9.4 1.2 %copy-done.1 = bf16[512,1024]{1,0:T(8,128)(2,1)S(1)} copy-done((bf16[512,1024]{1,0:T(8,128)(2,1)S(1)}, bf16[512,1024]{1,0:T(8,128)(2,1)}, u32[]{:S(2)}) %copy-start.1) | copy-done | bytes 1048600
  10.6 2.1 %pack_beta.1 = (bf16[512,512]{1,0:T(8,128)(2,1)}, bf16[512,512]{1,0:T(8,128)(2,1)}, bf16[512,512]{1,0:T(8,128)(2,1)}) custom-call(s32[12]{0:T(128)S(1)} %reshape.155.pack_ref, bf16[512,1024]{1,0:T(8,128)(2,1)S(1)} %copy-done.1), custom_call_target="tpu_custom_call" | custom-call | tf_op jit(solution)/shard_map/pack_beta/pallas_call | solution.py:68
  12.7 1.5 %collective-permute-start.2 = (bf16[512,512]{1,0:T(8,128)(2,1)}, bf16[512,512]{1,0:T(8,128)(2,1)S(1)}, u32[]{:S(2)}, u32[]{:S(2)}) collective-permute-start(bf16[512,512]{1,0:T(8,128)(2,1)} %get-tuple-element.27), channel_id=1, source_target_pairs={{0,1},{1,0},{2,3},{3,2},{4,5},{5,4},{6,7},{7,6},{8,9},{9,8},{10,11... | collective-permute-start | bytes 1572872 | tf_op jit(solution)/shard_map/ppermute | solution.py:216
  14.2 1.5 %collective-permute-start.3 = (bf16[512,512]{1,0:T(8,128)(2,1)}, bf16[512,512]{1,0:T(8,128)(2,1)S(1)}, u32[]{:S(2)}, u32[]{:S(2)}) collective-permute-start(bf16[512,512]{1,0:T(8,128)(2,1)} %get-tuple-element.28), channel_id=1, source_target_pairs={{0,2},{1,3},{2,0},{3,1},{4,6},{5,7},{6,4},{7,5},{8,10},{9,11},{10,... | collective-permute-start | bytes 1572872 | tf_op jit(solution)/shard_map/ppermute | solution.py:216
  19.1 8.7 %collective-permute-done.2.rest_0_ = bf16[512,512]{1,0:T(8,128)(2,1)S(1)} collective-permute-done((bf16[512,512]{1,0:T(8,128)(2,1)}, bf16[512,512]{1,0:T(8,128)(2,1)S(1)}, u32[]{:S(2)}, u32[]{:S(2)}) %collective-permute-start.2) | collective-permute-done | bytes 524320 | tf_op jit(solution)/shard_map/ppermute | solution.py:216
  28.6 9.9 %collective-permute-done.3.rest_1_ = bf16[512,512]{1,0:T(8,128)(2,1)S(1)} collective-permute-done((bf16[512,512]{1,0:T(8,128)(2,1)}, bf16[512,512]{1,0:T(8,128)(2,1)S(1)}, u32[]{:S(2)}, u32[]{:S(2)}) %collective-permute-start.3) | collective-permute-done | bytes 524320 | tf_op jit(solution)/shard_map/ppermute | solution.py:216
  39.3 10.7 %collective-permute-done.1.rest_4_ = bf16[512,1024]{1,0:T(8,128)(2,1)S(1)} collective-permute-done((bf16[512,1024]{1,0:T(8,128)(2,1)}, bf16[512,1024]{1,0:T(8,128)(2,1)S(1)}, u32[]{:S(2)}, u32[]{:S(2)}) %collective-permute-start.1) | collective-permute-done | bytes 1048608 | tf_op jit(solution)/shard_map/ppermute | solution.py:160
  50.7 1.0 %copy-done.8 = bf16[512,1024]{1,0:T(8,128)(2,1)} copy-done((bf16[512,1024]{1,0:T(8,128)(2,1)}, bf16[512,1024]{1,0:T(8,128)(2,1)S(1)}, u32[]{:S(2)}) %copy-start.8) | copy-done | bytes 1048600
  51.7 1.5 %collective-permute-start.5 = (bf16[512,1024]{1,0:T(8,128)(2,1)S(1)}, bf16[512,1024]{1,0:T(8,128)(2,1)}, u32[]{:S(2)}, u32[]{:S(2)}) collective-permute-start(bf16[512,1024]{1,0:T(8,128)(2,1)S(1)} %collective-permute-done.1.rest_4_), channel_id=1, source_target_pairs={{0,8},{4,12},{8,0},{12,4},{16,24},{20,28},{24,16},{28,20},{1,9},{5... | collective-permute-start | bytes 3145736 | tf_op jit(solution)/shard_map/ppermute | solution.py:160
  53.3 1.2 %collective-permute-done.6.rest_5_ = bf16[512,1024]{1,0:T(8,128)(2,1)S(1)} collective-permute-done((bf16[512,1024]{1,0:T(8,128)(2,1)}, bf16[512,1024]{1,0:T(8,128)(2,1)S(1)}, u32[]{:S(2)}, u32[]{:S(2)}) %collective-permute-start.6) | collective-permute-done | bytes 1048608 | tf_op jit(solution)/shard_map/ppermute | solution.py:164
  54.5 1.0 %copy-done.10 = bf16[512,1024]{1,0:T(8,128)(2,1)} copy-done((bf16[512,1024]{1,0:T(8,128)(2,1)}, bf16[512,1024]{1,0:T(8,128)(2,1)S(1)}, u32[]{:S(2)}) %copy-start.10) | copy-done | bytes 1048600
  56.0 1.2 %copy-done.2 = bf16[512,1024]{1,0:T(8,128)(2,1)S(1)} copy-done((bf16[512,1024]{1,0:T(8,128)(2,1)S(1)}, bf16[512,1024]{1,0:T(8,128)(2,1)}, u32[]{:S(2)}) %copy-start.2) | copy-done | bytes 1048600
  57.2 2.0 %copy-done.6 = bf16[8,14,128,128]{3,2,1,0:T(8,128)(2,1)S(1)} copy-done((bf16[8,14,128,128]{3,2,1,0:T(8,128)(2,1)S(1)}, bf16[8,14,128,128]{3,2,1,0:T(8,128)(2,1)}, u32[]{:S(2)}) %copy-start.6) | copy-done | bytes 3670040
  59.2 1.6 %copy-done.7 = f32[512,1024]{1,0:T(8,128)S(1)} copy-done((f32[512,1024]{1,0:T(8,128)S(1)}, f32[512,1024]{1,0:T(8,128)}, u32[]{:S(2)}) %copy-start.7) | copy-done | bytes 2097176
  60.8 1.0 %copy-done.13 = bf16[512,512]{1,0:T(8,128)(2,1)S(1)} copy-done((bf16[512,512]{1,0:T(8,128)(2,1)S(1)}, bf16[512,512]{1,0:T(8,128)(2,1)}, u32[]{:S(2)}) %copy-start.13) | copy-done | bytes 524312
  61.9 1.0 %copy-done.15 = bf16[512,512]{1,0:T(8,128)(2,1)S(1)} copy-done((bf16[512,512]{1,0:T(8,128)(2,1)S(1)}, bf16[512,512]{1,0:T(8,128)(2,1)}, u32[]{:S(2)}) %copy-start.15) | copy-done | bytes 524312
  62.9 5.1 %beta_product.1.rest_1_ = f32[512,1024]{1,0:T(8,128)S(1)} custom-call(s32[160]{0:T(256)S(1)} %reshape.158.table_ref, bf16[8,14,128,128]{3,2,1,0:T(8,128)(2,1)S(1)} %copy-done.6, f32[512,1024]{1,0:T(8,128)S(1)} %copy-done.7, bf16[512,1024]{1,0:T(8,128)(2,1)S(1)} %copy-done.2, bf16[512,512]{1,0:T(8,128)(2,1)S(1)} %copy-done.13, ...), custom_call_target="tpu_custom_call" | custom-call | tf_op jit(solution)/shard_map/beta_product/pallas_call | solution.py:106
  68.0 5.6 %alpha_product.2.rest_1_ = f32[512,1024]{1,0:T(8,128)S(1)} custom-call(s32[96]{0:T(128)S(1)} %reshape.157.table_ref, bf16[4,14,128,128]{3,2,1,0:T(8,128)(2,1)S(1)} %copy-done.4, f32[512,1024]{1,0:T(8,128)S(1)} %beta_product.1.rest_1_, bf16[512,1024]{1,0:T(8,128)(2,1)S(1)} %copy-done.3, bf16[512,1024]{1,0:T(8,128)(2,1)S(1)} %copy-done.9, ...), custom_call_target="tpu_custom_call" | custom-call | tf_op jit(solution)/shard_map/alpha_product/pallas_call | solution.py:144
  73.7 3.7 %collective-permute-done.5.rest_2_ = bf16[512,1024]{1,0:T(8,128)(2,1)} collective-permute-done((bf16[512,1024]{1,0:T(8,128)(2,1)S(1)}, bf16[512,1024]{1,0:T(8,128)(2,1)}, u32[]{:S(2)}, u32[]{:S(2)}) %collective-permute-start.5) | collective-permute-done | bytes 1048608 | tf_op jit(solution)/shard_map/ppermute | solution.py:160
  77.4 2.8 %collective-permute-done.9.rest_3_ = bf16[512,1024]{1,0:T(8,128)(2,1)S(1)} collective-permute-done((bf16[512,1024]{1,0:T(8,128)(2,1)}, bf16[512,1024]{1,0:T(8,128)(2,1)S(1)}, u32[]{:S(2)}, u32[]{:S(2)}) %collective-permute-start.9) | collective-permute-done | bytes 1048608 | tf_op jit(solution)/shard_map/ppermute | solution.py:164
  80.2 1.5 %copy-done.5 = bf16[4,14,128,128]{3,2,1,0:T(8,128)(2,1)S(1)} copy-done((bf16[4,14,128,128]{3,2,1,0:T(8,128)(2,1)S(1)}, bf16[4,14,128,128]{3,2,1,0:T(8,128)(2,1)}, u32[]{:S(2)}) %copy-start.5) | copy-done | bytes 1835032
  81.7 4.0 %alpha_product.3 = bf16[512,1024]{1,0:T(8,128)(2,1)} custom-call(s32[32]{0:T(128)S(1)} %reshape.156.table_ref, bf16[4,14,128,128]{3,2,1,0:T(8,128)(2,1)S(1)} %copy-done.5, f32[512,1024]{1,0:T(8,128)S(1)} %alpha_product.2.rest_1_, bf16[512,1024]{1,0:T(8,128)(2,1)} %collective-permute-done.5.rest_2_, bf16[512,1024]{1,0:T(8,128)(2,1)S(1)} %collective-permute-done.9.rest_3_), custom_call_target="tpu_custom_call" | custom-call | tf_op jit(solution)/shard_map/alpha_product/pallas_call | solution.py:144
  (64 shorter events, 10.2 us)
Async XLA Ops:
  0.0 16.2 %copy-start = (s32[32,14]{0,1:T(8,128)S(1)}, s32[32,14]{0,1:T(8,128)}, u32[]{:S(2)}) copy-start(s32[32,14]{0,1:T(8,128)} %param.14) | copy-start | bytes 5380
  0.0 50.0 %collective-permute-start.1 = (bf16[512,1024]{1,0:T(8,128)(2,1)}, bf16[512,1024]{1,0:T(8,128)(2,1)S(1)}, u32[]{:S(2)}, u32[]{:S(2)}) collective-permute-start(bf16[512,1024]{1,0:T(8,128)(2,1)} %rest_2_), channel_id=1, source_target_pairs={{0,16},{4,20},{8,24},{12,28},{16,0},{20,4},{24,8},{28,12},{1,17},{... | collective-permute-start | bytes 3145736 | tf_op jit(solution)/shard_map/ppermute | solution.py:160
  4.0 46.1 %collective-permute-start = (bf16[512,1024]{1,0:T(8,128)(2,1)}, bf16[512,1024]{1,0:T(8,128)(2,1)S(1)}, u32[]{:S(2)}, u32[]{:S(2)}) collective-permute-start(bf16[512,1024]{1,0:T(8,128)(2,1)} %rest_2_), channel_id=1, source_target_pairs={{0,8},{4,12},{8,0},{12,4},{16,24},{20,28},{24,16},{28,20},{1,9},{5... | collective-permute-start | bytes 3145736 | tf_op jit(solution)/shard_map/ppermute | solution.py:160
  9.4 1.2 %copy-start.1 = (bf16[512,1024]{1,0:T(8,128)(2,1)S(1)}, bf16[512,1024]{1,0:T(8,128)(2,1)}, u32[]{:S(2)}) copy-start(bf16[512,1024]{1,0:T(8,128)(2,1)} %rest_2_) | copy-start | bytes 3145732
  12.7 15.1 %collective-permute-start.2 = (bf16[512,512]{1,0:T(8,128)(2,1)}, bf16[512,512]{1,0:T(8,128)(2,1)S(1)}, u32[]{:S(2)}, u32[]{:S(2)}) collective-permute-start(bf16[512,512]{1,0:T(8,128)(2,1)} %get-tuple-element.27), channel_id=1, source_target_pairs={{0,1},{1,0},{2,3},{3,2},{4,5},{5,4},{6,7},{7,6},{8,9},{9,8},{10,11... | collective-permute-start | bytes 1572872 | tf_op jit(solution)/shard_map/ppermute | solution.py:216
  14.2 24.3 %collective-permute-start.3 = (bf16[512,512]{1,0:T(8,128)(2,1)}, bf16[512,512]{1,0:T(8,128)(2,1)S(1)}, u32[]{:S(2)}, u32[]{:S(2)}) collective-permute-start(bf16[512,512]{1,0:T(8,128)(2,1)} %get-tuple-element.28), channel_id=1, source_target_pairs={{0,2},{1,3},{2,0},{3,1},{4,6},{5,7},{6,4},{7,5},{8,10},{9,11},{10,... | collective-permute-start | bytes 1572872 | tf_op jit(solution)/shard_map/ppermute | solution.py:216
  15.7 23.6 %collective-permute-start.4 = (bf16[512,512]{1,0:T(8,128)(2,1)}, bf16[512,512]{1,0:T(8,128)(2,1)}, u32[]{:S(2)}, u32[]{:S(2)}) collective-permute-start(bf16[512,512]{1,0:T(8,128)(2,1)} %get-tuple-element.29), channel_id=1, source_target_pairs={{0,3},{1,2},{2,1},{3,0},{4,7},{5,6},{6,5},{7,4},{8,11},{9,10},{10,... | collective-permute-start | bytes 1572872 | tf_op jit(solution)/shard_map/ppermute | solution.py:216
  50.2 4.3 %collective-permute-start.6 = (bf16[512,1024]{1,0:T(8,128)(2,1)}, bf16[512,1024]{1,0:T(8,128)(2,1)S(1)}, u32[]{:S(2)}, u32[]{:S(2)}) collective-permute-start(bf16[512,1024]{1,0:T(8,128)(2,1)} %rest_2_), channel_id=1, source_target_pairs={{0,4},{4,0},{8,12},{12,8},{16,20},{20,16},{24,28},{28,24},{1,5},{5... | collective-permute-start | bytes 3145736 | tf_op jit(solution)/shard_map/ppermute | solution.py:164
  50.2 5.3 %collective-permute-start.7 = (bf16[512,1024]{1,0:T(8,128)(2,1)S(1)}, bf16[512,1024]{1,0:T(8,128)(2,1)}, u32[]{:S(2)}, u32[]{:S(2)}) collective-permute-start(bf16[512,1024]{1,0:T(8,128)(2,1)S(1)} %collective-permute-done.rest_3_), channel_id=1, source_target_pairs={{0,4},{4,0},{8,12},{12,8},{16,20},{20,16},{24,28},{28,24},{1,5},{5... | collective-permute-start | bytes 3145736 | tf_op jit(solution)/shard_map/ppermute | solution.py:164
  50.7 1.0 %copy-start.8 = (bf16[512,1024]{1,0:T(8,128)(2,1)}, bf16[512,1024]{1,0:T(8,128)(2,1)S(1)}, u32[]{:S(2)}) copy-start(bf16[512,1024]{1,0:T(8,128)(2,1)S(1)} %collective-permute-done.rest_3_) | copy-start | bytes 3145732
  51.7 4.3 %collective-permute-start.8 = (bf16[512,1024]{1,0:T(8,128)(2,1)S(1)}, bf16[512,1024]{1,0:T(8,128)(2,1)}, u32[]{:S(2)}, u32[]{:S(2)}) collective-permute-start(bf16[512,1024]{1,0:T(8,128)(2,1)S(1)} %collective-permute-done.1.rest_4_), channel_id=1, source_target_pairs={{0,4},{4,0},{8,12},{12,8},{16,20},{20,16},{24,28},{28,24},{1,5},{5... | collective-permute-start | bytes 3145736 | tf_op jit(solution)/shard_map/ppermute | solution.py:164
  51.7 25.7 %collective-permute-start.5 = (bf16[512,1024]{1,0:T(8,128)(2,1)S(1)}, bf16[512,1024]{1,0:T(8,128)(2,1)}, u32[]{:S(2)}, u32[]{:S(2)}) collective-permute-start(bf16[512,1024]{1,0:T(8,128)(2,1)S(1)} %collective-permute-done.1.rest_4_), channel_id=1, source_target_pairs={{0,8},{4,12},{8,0},{12,4},{16,24},{20,28},{24,16},{28,20},{1,9},{5... | collective-permute-start | bytes 3145736 | tf_op jit(solution)/shard_map/ppermute | solution.py:160
  54.5 1.0 %copy-start.10 = (bf16[512,1024]{1,0:T(8,128)(2,1)}, bf16[512,1024]{1,0:T(8,128)(2,1)S(1)}, u32[]{:S(2)}) copy-start(bf16[512,1024]{1,0:T(8,128)(2,1)S(1)} %collective-permute-done.6.rest_5_) | copy-start | bytes 3145732
  56.0 1.2 %copy-start.2 = (bf16[512,1024]{1,0:T(8,128)(2,1)S(1)}, bf16[512,1024]{1,0:T(8,128)(2,1)}, u32[]{:S(2)}) copy-start(bf16[512,1024]{1,0:T(8,128)(2,1)} %rest_2_) | copy-start | bytes 3145732
  57.2 2.0 %copy-start.6 = (bf16[8,14,128,128]{3,2,1,0:T(8,128)(2,1)S(1)}, bf16[8,14,128,128]{3,2,1,0:T(8,128)(2,1)}, u32[]{:S(2)}) copy-start(bf16[8,14,128,128]{3,2,1,0:T(8,128)(2,1)} %h_ref.1) | copy-start | bytes 11010052
  59.2 1.6 %copy-start.7 = (f32[512,1024]{1,0:T(8,128)S(1)}, f32[512,1024]{1,0:T(8,128)}, u32[]{:S(2)}) copy-start(f32[512,1024]{1,0:T(8,128)} %d_ref.1) | copy-start | bytes 6291460
  60.8 1.0 %copy-start.13 = (bf16[512,512]{1,0:T(8,128)(2,1)S(1)}, bf16[512,512]{1,0:T(8,128)(2,1)}, u32[]{:S(2)}) copy-start(bf16[512,512]{1,0:T(8,128)(2,1)} %copy-done.12) | copy-start | bytes 1572868
  61.9 1.0 %copy-start.15 = (bf16[512,512]{1,0:T(8,128)(2,1)S(1)}, bf16[512,512]{1,0:T(8,128)(2,1)}, u32[]{:S(2)}) copy-start(bf16[512,512]{1,0:T(8,128)(2,1)} %copy-done.14) | copy-start | bytes 1572868
  62.9 5.1 %copy-start.3 = (bf16[512,1024]{1,0:T(8,128)(2,1)S(1)}, bf16[512,1024]{1,0:T(8,128)(2,1)}, u32[]{:S(2)}) copy-start(bf16[512,1024]{1,0:T(8,128)(2,1)} %rest_2_) | copy-start | bytes 3145732
  62.9 5.1 %copy-start.4 = (bf16[4,14,128,128]{3,2,1,0:T(8,128)(2,1)S(1)}, bf16[4,14,128,128]{3,2,1,0:T(8,128)(2,1)}, u32[]{:S(2)}) copy-start(bf16[4,14,128,128]{3,2,1,0:T(8,128)(2,1)} %rest_0_.3) | copy-start | bytes 5505028
  62.9 5.1 %copy-start.9 = (bf16[512,1024]{1,0:T(8,128)(2,1)S(1)}, bf16[512,1024]{1,0:T(8,128)(2,1)}, u32[]{:S(2)}) copy-start(bf16[512,1024]{1,0:T(8,128)(2,1)} %copy-done.8) | copy-start | bytes 3145732
  62.9 5.1 %copy-start.11 = (bf16[512,1024]{1,0:T(8,128)(2,1)S(1)}, bf16[512,1024]{1,0:T(8,128)(2,1)}, u32[]{:S(2)}) copy-start(bf16[512,1024]{1,0:T(8,128)(2,1)} %copy-done.10) | copy-start | bytes 3145732
  77.3 2.9 %collective-permute-start.9 = (bf16[512,1024]{1,0:T(8,128)(2,1)}, bf16[512,1024]{1,0:T(8,128)(2,1)S(1)}, u32[]{:S(2)}, u32[]{:S(2)}) collective-permute-start(bf16[512,1024]{1,0:T(8,128)(2,1)} %collective-permute-done.5.rest_2_), channel_id=1, source_target_pairs={{0,4},{4,0},{8,12},{12,8},{16,20},{20,16},{24,28},{28,24},{1,5},{5... | collective-permute-start | bytes 3145736 | tf_op jit(solution)/shard_map/ppermute | solution.py:164
  80.2 1.5 %copy-start.5 = (bf16[4,14,128,128]{3,2,1,0:T(8,128)(2,1)S(1)}, bf16[4,14,128,128]{3,2,1,0:T(8,128)(2,1)}, u32[]{:S(2)}) copy-start(bf16[4,14,128,128]{3,2,1,0:T(8,128)(2,1)} %rest_0_.3) | copy-start | bytes 5505028
  (2 other events, 1.6 us)

commit v2 on v1

--- a/solution.py
+++ b/solution.py
@@ -10,7 +10,6 @@
 
 CAP_B = 4
 CORES = 2
-STEP = 1
 VMEM_LIMIT = 40 * 1024 * 1024
 
 
@@ -79,11 +78,11 @@
     )(pack, coefficients)
 
 
-def fill(weights, table_ref, h_ref, rows, positions, block, first=0):
-    for i in range(first, first + rows):
+def fill(weights, table_ref, h_ref, rows, positions, block):
+    for i in range(rows):
         for q in range(positions):
             k = table_ref[i * positions + q]
-            tile = h_ref[i - first, jnp.maximum(k, 0)]
+            tile = h_ref[i, jnp.maximum(k, 0)]
             weights[i * block : (i + 1) * block, q * block : (q + 1) * block] = jnp.where(
                 k >= 0, tile, jnp.zeros_like(tile)
             )
@@ -118,42 +117,41 @@
     )(table.reshape(-1), beta_blocks, diagonal, coefficients, *arrived)
 
 
-def alpha_body(rows, positions, block, table_ref, h_refs, add_refs, piece_refs, out_refs, weights):
-    for n, h_ref in enumerate(h_refs):
-        fill(weights, table_ref, h_ref, rows, positions, block, n * rows)
-    x = jnp.concatenate([p[...] for p in piece_refs], axis=0)
-    height = rows * block
-    for n, out_ref in enumerate(out_refs):
-        total = jnp.dot(weights[n * height : (n + 1) * height], x, preferred_element_type=jnp.float32)
-        if add_refs:
-            total = total + add_refs[n][...]
-        out_ref[...] = total.astype(out_ref.dtype)
-
-
-def alpha_product(table, blocks, adds, pieces, dtype):
-    rows, block = blocks[0].shape[0], blocks[0].shape[2]
+def lay_out(table, blocks):
+    rows, block = blocks.shape[0], blocks.shape[2]
     positions = table.shape[1]
-    height, width = rows * block, pieces[0].shape[1]
-
-    def body(table_ref, *rest):
-        h_refs, rest = rest[: len(blocks)], rest[len(blocks) :]
-        add_refs, rest = rest[: len(adds)], rest[len(adds) :]
-        piece_refs, rest = rest[: len(pieces)], rest[len(pieces) :]
-        alpha_body(rows, positions, block, table_ref, h_refs, add_refs, piece_refs, rest[:-1], rest[-1])
+
+    def body(table_ref, h_ref, out_ref):
+        fill(out_ref, table_ref, h_ref, rows, positions, block)
 
     return pl.pallas_call(
         body,
         grid_spec=pltpu.PrefetchScalarGridSpec(
             num_scalar_prefetch=1,
             grid=(),
-            in_specs=[pl.BlockSpec(memory_space=pltpu.VMEM)] * (len(blocks) + len(adds) + len(pieces)),
-            out_specs=[pl.BlockSpec(memory_space=pltpu.VMEM)] * len(blocks),
-            scratch_shapes=[pltpu.VMEM((len(blocks) * height, positions * block), jnp.bfloat16)],
+            in_specs=[pl.BlockSpec(memory_space=pltpu.VMEM)],
+            out_specs=pl.BlockSpec(memory_space=pltpu.VMEM),
         ),
-        out_shape=[jax.ShapeDtypeStruct((height, width), dtype)] * len(blocks),
+        out_shape=jax.ShapeDtypeStruct((rows * block, positions * block), blocks.dtype),
+        compiler_params=pltpu.CompilerParams(vmem_limit_bytes=VMEM_LIMIT),
+        name="lay_out",
+    )(table.reshape(-1), blocks)
+
+
+def alpha_product(weights, pieces, acc, dtype):
+    def body(w_ref, acc_ref, *rest):
+        x = jnp.concatenate([p[...] for p in rest[:-1]], axis=0)
+        total = acc_ref[...] + jnp.dot(w_ref[...], x, preferred_element_type=jnp.float32)
+        rest[-1][...] = total.astype(dtype)
+
+    return pl.pallas_call(
+        body,
+        in_specs=[pl.BlockSpec(memory_space=pltpu.VMEM)] * (2 + len(pieces)),
+        out_specs=pl.BlockSpec(memory_space=pltpu.VMEM),
+        out_shape=jax.ShapeDtypeStruct(acc.shape, dtype),
         compiler_params=pltpu.CompilerParams(vmem_limit_bytes=VMEM_LIMIT),
         name="alpha_product",
-    )(table.reshape(-1), *blocks, *adds, *pieces)
+    )(weights, acc, *pieces)
 
 
 def send(x, edges):
@@ -184,10 +182,6 @@
     chips = lax.axis_size("alpha") // CORES
     owners_b = lax.axis_size("beta")
     index_a, index_b = lax.axis_index("alpha"), lax.axis_index("beta")
-    core = lax.rem(index_a, CORES)
-    height = rows_a * block
-    span = STEP * block
-    cuts = rows_a // STEP
 
     pack, beta_ids = beta_tables(beta_lists, index_b, owners_b, rows_b)
     mine_b = lax.dynamic_slice_in_dim(beta_lists, index_b * rows_b, rows_b, 0)
@@ -195,16 +189,13 @@
     def place(chip, first, count):
         return [(chip, first + g) if 0 <= chip < chips else None for g in range(count)]
 
-    def table_of(places, lists, swapped):
+    mine_a = lax.dynamic_slice_in_dim(alpha_lists, index_a * rows_a, rows_a, 0)
+
+    def table_of(places):
         ids = [block_ids(p, rows_a) for p in places]
-        if swapped:
-            ids = ids + [i[:, ::-1] for i in ids]
-        ids = jnp.asarray(np.concatenate(ids, axis=2).reshape(chips * CORES, -1))
-        return slot_table(lists, lax.dynamic_index_in_dim(ids, index_a, 0, keepdims=False))
-
-    mine_a = lax.dynamic_slice_in_dim(alpha_lists, index_a * rows_a, rows_a, 0)
-    theirs_a = lax.dynamic_slice_in_dim(alpha_lists, (index_a + 1 - 2 * core) * rows_a, rows_a, 0)
-    both = jnp.concatenate([mine_a, theirs_a], axis=0)
+        ids = jnp.asarray(np.concatenate(ids + [i[:, ::-1] for i in ids], axis=2).reshape(chips * CORES, -1))
+        return slot_table(mine_a, lax.dynamic_index_in_dim(ids, index_a, 0, keepdims=False))
+
     table_b = slot_table(mine_b, beta_ids)
 
     def beta_all(arrived):
@@ -216,60 +207,56 @@
             lax.ppermute(packed[s - 1], "beta", [(d, partner(d, s, owners_b)) for d in range(owners_b)]) for s in steps
         ]
 
-    def product(table, pieces, adds):
-        return alpha_product(table, [alpha_blocks, other_blocks], adds, pieces, jnp.float32)
-
-    def last_product(table, pieces, acc):
-        return alpha_product(table, [alpha_blocks], [acc], pieces, jnp.bfloat16)[0]
-
     everyone = range(chips)
     own = [place(p, 0, rows_a) for p in everyone]
     if chips == 4:
         far, near = [(0, 2), (1, 3), (2, 0), (3, 1)], [(0, 1), (1, 0), (2, 3), (3, 2)]
         far_from, near_from, both_from = [2, 3, 0, 1], [1, 0, 3, 2], [3, 2, 1, 0]
 
+
         def of(chip_of):
             return [place(chip_of[p], 0, rows_a) for p in everyone]
 
-        table_here = table_of([own, of(near_from), of(far_from)], mine_a, True)
-        table_both = table_of([of(both_from)], mine_a, True)
+        table_here = table_of([own, of(near_from), of(far_from)])
+        table_both = table_of([of(both_from)])
+        half = table_both.shape[1] // 2
 
         near_own, far_own = send(coefficients, near), send(coefficients, far)
         arrived = exchange(pack_beta(pack, coefficients, owners_b - 1, block))
-        near_own, far_own, here, table_here, table_both, table_b, *arrived = gate(
-            near_own, far_own, coefficients, table_here, table_both, table_b, *arrived
+        own_swapped = swap(coefficients, everyone)
+        near_own, far_own, own_swapped, here, table_here, table_b, table_same, table_other, *arrived = gate(
+            near_own, far_own, own_swapped, coefficients, table_here, table_b, table_both[:, :half], table_both[:, half:], *arrived
         )
 
         near_far = send(far_own, near)
         pieces = [here, near_own, far_own]
-        pieces += [swap(x, everyone) for x in pieces]
-        *pieces, here = gate(*pieces, here)
+        pieces += [own_swapped, swap(near_own, everyone), swap(far_own, everyone)]
+        *pieces, here, blocks_here = gate(*pieces, here, alpha_blocks)
         acc = beta_product(table_b, beta_blocks, here, diagonal, arrived)
-        (acc,) = alpha_product(table_here, [alpha_blocks], [acc], pieces, jnp.float32)
-        near_far, acc = gate(near_far, acc)
-        return last_product(table_both, [near_far, swap(near_far, everyone)], acc)
-
-    other_blocks = swap(alpha_blocks, everyone)
+        weights = [lay_out(table, blocks_here) for table in (table_here, table_same, table_other)]
+        acc = alpha_product(weights[0], pieces, acc, jnp.float32)
+        near_far, acc, *weights = gate(near_far, acc, *weights)
+        acc = alpha_product(weights[1], [near_far], acc, jnp.float32)
+        return alpha_product(weights[2], [swap(near_far, everyone)], acc, jnp.bfloat16)
+
     arrived = exchange(pack_beta(pack, coefficients, owners_b - 1, block))
     pieces, places = [coefficients], [own]
     left, right = [], []
-    for u in range((chips - 1) * cuts):
-        kind, v = u // cuts, u % cuts
-        mine = coefficients[v * span : (v + 1) * span]
-        left.append(send(mine if u < cuts else left[u - cuts], [(p, p - 1) for p in range(1, chips) if kind < chips - p]))
-        right.append(send(mine if u < cuts else right[u - cuts], [(p, p + 1) for p in range(chips - 1) if kind < p + 1]))
+    for u in range((chips - 1) * rows_a):
+        kind, v = u // rows_a, u % rows_a
+        mine = coefficients[v * block : (v + 1) * block]
+        left.append(send(mine if u < rows_a else left[u - rows_a], [(p, p - 1) for p in range(1, chips) if kind < chips - p]))
+        right.append(send(mine if u < rows_a else right[u - rows_a], [(p, p + 1) for p in range(chips - 1) if kind < p + 1]))
         pieces += [left[u], right[u]]
-        places += [
-            [place(p + 1 + kind, v * STEP, STEP) for p in everyone],
-            [place(p - 1 - kind, v * STEP, STEP) for p in everyone],
-        ]
-    sums = []
-    for k in range(0, len(pieces) - 2, 4):
-        upto = min(k + 4, len(pieces) - 2)
-        sums = product(table_of(places[k:upto], both, False), pieces[k:upto], sums)
-    acc = beta_all(arrived) + sums[0] + swap(sums[1], everyone)
-    ends = pieces[-2:]
-    return last_product(table_of(places[-2:], mine_a, True), ends + [swap(x, everyone) for x in ends], acc)
+        places += [[place(p + 1 + kind, v, 1) for p in everyone], [place(p - 1 - kind, v, 1) for p in everyone]]
+    acc = beta_product(table_b, beta_blocks, coefficients, diagonal, arrived)
+    step = 2 * rows_a
+    for k in range(0, len(pieces), step):
+        last = k + step >= len(pieces)
+        weights = lay_out(table_of(places[k : k + step]), alpha_blocks)
+        xs = pieces[k : k + step] + [swap(x, everyone) for x in pieces[k : k + step]]
+        acc = alpha_product(weights, xs, acc, jnp.bfloat16 if last else jnp.float32)
+    return acc
 
 
 def solution(mesh):

time: 86.3 us -> 82.6 us (0.957)
  local copies, waits for them, and re-layouts: 18.2 us -> 13.6 us
  starting transfers between devices: 11.1 us -> 12 us
    unnamed x33 -> x29, local copies, waits for them, and re-layouts: 14.1 us -> 9.3 us
    ppermute x3, starting transfers between devices: 3.49 us -> 5.46 us  [exchange(): lax.ppermute(packed[s - 1], 'beta', [(d, partner(d, s, owners_b)) for d i...]
    ppermute x3, waiting for transfers between devices: 14.5 us -> 13 us  [send(): lax.ppermute(x, 'alpha', [(s * CORES + c, t * CORES + c) for s, t in edge...]
    ppermute x3, waiting for transfers between devices: 18.6 us -> 20.1 us  [exchange(): lax.ppermute(packed[s - 1], 'beta', [(d, partner(d, s, owners_b)) for d i...]
    pallas_call x1, Pallas kernels: 5.08 us -> 3.76 us  [beta_product(): pl.pallas_call(functools.partial(beta_body, rows, positions, block), grid...]
    ppermute x3, starting transfers between devices: 7.1 us -> 6.04 us  [send(): lax.ppermute(x, 'alpha', [(s * CORES + c, t * CORES + c) for s, t in edge...]
    pallas_call x2 -> x6, Pallas kernels: 9.66 us -> 10.5 us  [the longest x3 7.69 us: alpha_product(): pl.pallas_call(body, in_specs=[pl.BlockSpec(memory_space=pltpu.VMEM)] * (...]
  transfers between devices with their start and end apart: 10 -> 10, of which waited for: 8 -> 7; matrix products, arithmetic and copies ran while one was open for 8% -> 9% of each run, Pallas kernels for 15% -> 18%
where the time goes in v2:
time: 82.6 us; the launch traced here: 82.2 us
  waiting for transfers between devices  38.3 us (46%)
  Pallas kernels  16.2 us (20%)
  local copies, waits for them, and re-layouts  13.6 us (16%)
  starting transfers between devices  12 us (15%)
  other arithmetic  1.99 us (2%)
    ppermute x3, waiting for transfers between devices, exchange(): lax.ppermute(packed[s - 1], 'beta', [(d, partner(d, s, owners_b)) for d i...  20.1 us
    ppermute x3, waiting for transfers between devices, send(): lax.ppermute(x, 'alpha', [(s * CORES + c, t * CORES + c) for s, t in edge...  13 us
    unnamed x29, local copies, waits for them, and re-layouts  9.3 us
    pallas_call x3, Pallas kernels, alpha_product(): pl.pallas_call(body, in_specs=[pl.BlockSpec(memory_space=pltpu.VMEM)] * (...  7.69 us
    ppermute x3, starting transfers between devices, send(): lax.ppermute(x, 'alpha', [(s * CORES + c, t * CORES + c) for s, t in edge...  6.04 us
    ppermute x3, starting transfers between devices, exchange(): lax.ppermute(packed[s - 1], 'beta', [(d, partner(d, s, owners_b)) for d i...  5.46 us
    ppermute x4, waiting for transfers between devices, swap(): lax.ppermute(x, 'alpha', [(p * CORES + c, p * CORES + 1 - c) for p in chi...  5.15 us
    pallas_call x1, Pallas kernels, beta_product(): pl.pallas_call(functools.partial(beta_body, rows, positions, block), grid...  3.76 us
  transfers between devices with their start and end apart: 10, of which 7 were waited for; matrix products, arithmetic and copies ran while one was open for 9% of the time, Pallas kernels for 18%

profile of v2, /device:TPU:0, one launch (start us, length us, event | category | flops | bytes accessed | tf_op | source)
XLA Modules:
  0.0 82.2 jit_solution(1358127715292898077)
XLA Ops:
  0.0 3.0 %collective-permute-start = (bf16[512,1024]{1,0:T(8,128)(2,1)}, bf16[512,1024]{1,0:T(8,128)(2,1)}, u32[]{:S(2)}, u32[]{:S(2)}) collective-permute-start(bf16[512,1024]{1,0:T(8,128)(2,1)} %rest_0_), channel_id=1, source_target_pairs={{0,8},{4,12},{8,0},{12,4},{16,24},{20,28},{24,16},{28,20},{1,9},{5... | collective-permute-start | bytes 3145736 | tf_op jit(solution)/shard_map/ppermute | solution.py:158
  3.0 2.6 %collective-permute-start.1 = (bf16[512,1024]{1,0:T(8,128)(2,1)}, bf16[512,1024]{1,0:T(8,128)(2,1)S(1)}, u32[]{:S(2)}, u32[]{:S(2)}) collective-permute-start(bf16[512,1024]{1,0:T(8,128)(2,1)} %rest_0_), channel_id=1, source_target_pairs={{0,16},{4,20},{8,24},{12,28},{16,0},{20,4},{24,8},{28,12},{1,17},{... | collective-permute-start | bytes 3145736 | tf_op jit(solution)/shard_map/ppermute | solution.py:158
  9.4 1.2 %copy-done.3 = bf16[512,1024]{1,0:T(8,128)(2,1)S(1)} copy-done((bf16[512,1024]{1,0:T(8,128)(2,1)S(1)}, bf16[512,1024]{1,0:T(8,128)(2,1)}, u32[]{:S(2)}) %copy-start.3) | copy-done | bytes 1048600
  10.6 1.9 %pack_beta.1 = (bf16[512,512]{1,0:T(8,128)(2,1)}, bf16[512,512]{1,0:T(8,128)(2,1)}, bf16[512,512]{1,0:T(8,128)(2,1)S(1)}) custom-call(s32[12]{0:T(128)S(1)} %reshape.158.pack_ref, bf16[512,1024]{1,0:T(8,128)(2,1)S(1)} %copy-done.3), custom_call_target="tpu_custom_call" | custom-call | tf_op jit(solution)/shard_map/pack_beta/pallas_call | solution.py:67
  12.6 0.8 %copy-done.13 = bf16[512,512]{1,0:T(8,128)(2,1)} copy-done((bf16[512,512]{1,0:T(8,128)(2,1)}, bf16[512,512]{1,0:T(8,128)(2,1)S(1)}, u32[]{:S(2)}) %copy-start.13) | copy-done | bytes 524312
  13.4 1.5 %collective-permute-start.3 = (bf16[512,512]{1,0:T(8,128)(2,1)}, bf16[512,512]{1,0:T(8,128)(2,1)S(1)}, u32[]{:S(2)}, u32[]{:S(2)}) collective-permute-start(bf16[512,512]{1,0:T(8,128)(2,1)} %get-tuple-element.32), channel_id=1, source_target_pairs={{0,1},{1,0},{2,3},{3,2},{4,5},{5,4},{6,7},{7,6},{8,9},{9,8},{10,11... | collective-permute-start | bytes 1572872 | tf_op jit(solution)/shard_map/ppermute | solution.py:207
  14.9 1.5 %collective-permute-start.4 = (bf16[512,512]{1,0:T(8,128)(2,1)}, bf16[512,512]{1,0:T(8,128)(2,1)S(1)}, u32[]{:S(2)}, u32[]{:S(2)}) collective-permute-start(bf16[512,512]{1,0:T(8,128)(2,1)} %get-tuple-element.33), channel_id=1, source_target_pairs={{0,2},{1,3},{2,0},{3,1},{4,6},{5,7},{6,4},{7,5},{8,10},{9,11},{10,... | collective-permute-start | bytes 1572872 | tf_op jit(solution)/shard_map/ppermute | solution.py:207
  19.0 8.9 %collective-permute-done.3.rest_0_ = bf16[512,512]{1,0:T(8,128)(2,1)S(1)} collective-permute-done((bf16[512,512]{1,0:T(8,128)(2,1)}, bf16[512,512]{1,0:T(8,128)(2,1)S(1)}, u32[]{:S(2)}, u32[]{:S(2)}) %collective-permute-start.3) | collective-permute-done | bytes 524320 | tf_op jit(solution)/shard_map/ppermute | solution.py:207
  27.9 2.4 %collective-permute-start.5 = (bf16[512,512]{1,0:T(8,128)(2,1)}, bf16[512,512]{1,0:T(8,128)(2,1)S(1)}, u32[]{:S(2)}, u32[]{:S(2)}) collective-permute-start(bf16[512,512]{1,0:T(8,128)(2,1)} %copy-done.13), channel_id=1, source_target_pairs={{0,3},{1,2},{2,1},{3,0},{4,7},{5,6},{6,5},{7,4},{8,11},{9,10},{10,... | collective-permute-start | bytes 1572872 | tf_op jit(solution)/shard_map/ppermute | solution.py:207
  30.7 0.8 copy-done.9
  31.5 11.2 %collective-permute-done.5.rest_2_ = bf16[512,512]{1,0:T(8,128)(2,1)S(1)} collective-permute-done((bf16[512,512]{1,0:T(8,128)(2,1)}, bf16[512,512]{1,0:T(8,128)(2,1)S(1)}, u32[]{:S(2)}, u32[]{:S(2)}) %collective-permute-start.5) | collective-permute-done | bytes 524320 | tf_op jit(solution)/shard_map/ppermute | solution.py:207
  42.7 0.8 copy-done.11
  43.5 5.4 %collective-permute-done.rest_1_ = bf16[512,1024]{1,0:T(8,128)(2,1)} collective-permute-done((bf16[512,1024]{1,0:T(8,128)(2,1)}, bf16[512,1024]{1,0:T(8,128)(2,1)}, u32[]{:S(2)}, u32[]{:S(2)}) %collective-permute-start) | collective-permute-done | bytes 1048608 | tf_op jit(solution)/shard_map/ppermute | solution.py:158
  48.8 2.5 %collective-permute-done.1.rest_2_ = bf16[512,1024]{1,0:T(8,128)(2,1)S(1)} collective-permute-done((bf16[512,1024]{1,0:T(8,128)(2,1)}, bf16[512,1024]{1,0:T(8,128)(2,1)S(1)}, u32[]{:S(2)}, u32[]{:S(2)}) %collective-permute-start.1) | collective-permute-done | bytes 1048608 | tf_op jit(solution)/shard_map/ppermute | solution.py:158
  51.3 1.0 %copy-done.7 = bf16[512,1024]{1,0:T(8,128)(2,1)} copy-done((bf16[512,1024]{1,0:T(8,128)(2,1)}, bf16[512,1024]{1,0:T(8,128)(2,1)S(1)}, u32[]{:S(2)}) %copy-start.7) | copy-done | bytes 1048600
  53.5 3.2 %collective-permute-done.7.rest_4_ = bf16[512,1024]{1,0:T(8,128)(2,1)} collective-permute-done((bf16[512,1024]{1,0:T(8,128)(2,1)}, bf16[512,1024]{1,0:T(8,128)(2,1)}, u32[]{:S(2)}, u32[]{:S(2)}) %collective-permute-start.7) | collective-permute-done | bytes 1048608 | tf_op jit(solution)/shard_map/ppermute | solution.py:162
  56.7 1.5 %copy-done.1 = bf16[4,14,128,128]{3,2,1,0:T(8,128)(2,1)S(1)} copy-done((bf16[4,14,128,128]{3,2,1,0:T(8,128)(2,1)S(1)}, bf16[4,14,128,128]{3,2,1,0:T(8,128)(2,1)}, u32[]{:S(2)}) %copy-start.1) | copy-done | bytes 1835032
  58.2 1.5 %lay_out.3.w_ref = bf16[512,3072]{1,0:T(8,128)(2,1)S(1)} custom-call(s32[96]{0:T(128)S(1)} %reshape.159.table_ref, bf16[4,14,128,128]{3,2,1,0:T(8,128)(2,1)S(1)} %copy-done.1), custom_call_target="tpu_custom_call" | custom-call | tf_op jit(solution)/shard_map/lay_out/pallas_call | solution.py:127
  62.0 1.6 %copy-done.6 = f32[512,1024]{1,0:T(8,128)S(1)} copy-done((f32[512,1024]{1,0:T(8,128)S(1)}, f32[512,1024]{1,0:T(8,128)}, u32[]{:S(2)}) %copy-start.6) | copy-done | bytes 2097176
  63.5 3.8 %beta_product.1.acc_ref = f32[512,1024]{1,0:T(8,128)S(1)} custom-call(s32[160]{0:T(256)S(1)} %reshape.160.table_ref, bf16[8,14,128,128]{3,2,1,0:T(8,128)(2,1)S(1)} %copy-done.5, f32[512,1024]{1,0:T(8,128)S(1)} %copy-done.6, bf16[512,1024]{1,0:T(8,128)(2,1)S(1)} %copy-done.4, bf16[512,512]{1,0:T(8,128)(2,1)S(1)} %collective-permute-done.3.rest_0_, ...), custom_call_target="tpu_custom_call" | custom-call | tf_op jit(solution)/shard_map/beta_product/pallas_call | solution.py:105
  67.3 5.3 %alpha_product.3.acc_ref = f32[512,1024]{1,0:T(8,128)S(1)} custom-call(bf16[512,3072]{1,0:T(8,128)(2,1)S(1)} %lay_out.3.w_ref, f32[512,1024]{1,0:T(8,128)S(1)} %beta_product.1.acc_ref, bf16[512,1024]{1,0:T(8,128)(2,1)S(1)} %copy-done.4, bf16[512,1024]{1,0:T(8,128)(2,1)} %collective-permute-done.rest_1_, ...), custom_call_target="tpu_custom_call" | custom-call | tf_op jit(solution)/shard_map/alpha_product/pallas_call | solution.py:147
  72.6 5.2 %collective-permute-done.6.rest_0_ = bf16[512,1024]{1,0:T(8,128)(2,1)S(1)} collective-permute-done((bf16[512,1024]{1,0:T(8,128)(2,1)S(1)}, bf16[512,1024]{1,0:T(8,128)(2,1)S(1)}, u32[]{:S(2)}, u32[]{:S(2)}) %collective-permute-start.6) | collective-permute-done | bytes 1048608 | tf_op jit(solution)/shard_map/ppermute | solution.py:158
  78.6 1.9 %collective-permute-done.9.rest_0_ = bf16[512,1024]{1,0:T(8,128)(2,1)S(1)} collective-permute-done((bf16[512,1024]{1,0:T(8,128)(2,1)S(1)}, bf16[512,1024]{1,0:T(8,128)(2,1)S(1)}, u32[]{:S(2)}, u32[]{:S(2)}) %collective-permute-start.9) | collective-permute-done | bytes 1048608 | tf_op jit(solution)/shard_map/ppermute | solution.py:162
  80.5 1.7 %alpha_product.5 = bf16[512,1024]{1,0:T(8,128)(2,1)} custom-call(bf16[512,512]{1,0:T(8,128)(2,1)S(1)} %lay_out.5.w_ref, f32[512,1024]{1,0:T(8,128)S(1)} %alpha_product.4.acc_ref, bf16[512,1024]{1,0:T(8,128)(2,1)S(1)} %collective-permute-done.9.rest_0_), custom_call_target="tpu_custom_call" | custom-call | tf_op jit(solution)/shard_map/alpha_product/pallas_call | solution.py:147
  (66 shorter events, 10.9 us)
Async XLA Ops:
  0.0 16.4 %copy-start = (s32[32,14]{0,1:T(8,128)S(1)}, s32[32,14]{0,1:T(8,128)}, u32[]{:S(2)}) copy-start(s32[32,14]{0,1:T(8,128)} %param.14) | copy-start | bytes 5380
  0.0 48.8 %collective-permute-start = (bf16[512,1024]{1,0:T(8,128)(2,1)}, bf16[512,1024]{1,0:T(8,128)(2,1)}, u32[]{:S(2)}, u32[]{:S(2)}) collective-permute-start(bf16[512,1024]{1,0:T(8,128)(2,1)} %rest_0_), channel_id=1, source_target_pairs={{0,8},{4,12},{8,0},{12,4},{16,24},{20,28},{24,16},{28,20},{1,9},{5... | collective-permute-start | bytes 3145736 | tf_op jit(solution)/shard_map/ppermute | solution.py:158
  3.0 48.3 %collective-permute-start.1 = (bf16[512,1024]{1,0:T(8,128)(2,1)}, bf16[512,1024]{1,0:T(8,128)(2,1)S(1)}, u32[]{:S(2)}, u32[]{:S(2)}) collective-permute-start(bf16[512,1024]{1,0:T(8,128)(2,1)} %rest_0_), channel_id=1, source_target_pairs={{0,16},{4,20},{8,24},{12,28},{16,0},{20,4},{24,8},{28,12},{1,17},{... | collective-permute-start | bytes 3145736 | tf_op jit(solution)/shard_map/ppermute | solution.py:158
  5.6 45.7 %collective-permute-start.2 = (bf16[512,1024]{1,0:T(8,128)(2,1)}, bf16[512,1024]{1,0:T(8,128)(2,1)S(1)}, u32[]{:S(2)}, u32[]{:S(2)}) collective-permute-start(bf16[512,1024]{1,0:T(8,128)(2,1)} %rest_0_), channel_id=1, source_target_pairs={{0,4},{4,0},{8,12},{12,8},{16,20},{20,16},{24,28},{28,24},{1,5},{5... | collective-permute-start | bytes 3145736 | tf_op jit(solution)/shard_map/ppermute | solution.py:162
  9.4 1.2 %copy-start.3 = (bf16[512,1024]{1,0:T(8,128)(2,1)S(1)}, bf16[512,1024]{1,0:T(8,128)(2,1)}, u32[]{:S(2)}) copy-start(bf16[512,1024]{1,0:T(8,128)(2,1)} %rest_0_) | copy-start | bytes 3145732
  12.6 0.8 %copy-start.13 = (bf16[512,512]{1,0:T(8,128)(2,1)}, bf16[512,512]{1,0:T(8,128)(2,1)S(1)}, u32[]{:S(2)}) copy-start(bf16[512,512]{1,0:T(8,128)(2,1)S(1)} %get-tuple-element.34) | copy-start | bytes 1572868
  13.4 14.5 %collective-permute-start.3 = (bf16[512,512]{1,0:T(8,128)(2,1)}, bf16[512,512]{1,0:T(8,128)(2,1)S(1)}, u32[]{:S(2)}, u32[]{:S(2)}) collective-permute-start(bf16[512,512]{1,0:T(8,128)(2,1)} %get-tuple-element.32), channel_id=1, source_target_pairs={{0,1},{1,0},{2,3},{3,2},{4,5},{5,4},{6,7},{7,6},{8,9},{9,8},{10,11... | collective-permute-start | bytes 1572872 | tf_op jit(solution)/shard_map/ppermute | solution.py:207
  14.9 15.8 %collective-permute-start.4 = (bf16[512,512]{1,0:T(8,128)(2,1)}, bf16[512,512]{1,0:T(8,128)(2,1)S(1)}, u32[]{:S(2)}, u32[]{:S(2)}) collective-permute-start(bf16[512,512]{1,0:T(8,128)(2,1)} %get-tuple-element.33), channel_id=1, source_target_pairs={{0,2},{1,3},{2,0},{3,1},{4,6},{5,7},{6,4},{7,5},{8,10},{9,11},{10,... | collective-permute-start | bytes 1572872 | tf_op jit(solution)/shard_map/ppermute | solution.py:207
  27.9 14.8 %collective-permute-start.5 = (bf16[512,512]{1,0:T(8,128)(2,1)}, bf16[512,512]{1,0:T(8,128)(2,1)S(1)}, u32[]{:S(2)}, u32[]{:S(2)}) collective-permute-start(bf16[512,512]{1,0:T(8,128)(2,1)} %copy-done.13), channel_id=1, source_target_pairs={{0,3},{1,2},{2,1},{3,0},{4,7},{5,6},{6,5},{7,4},{8,11},{9,10},{10,... | collective-permute-start | bytes 1572872 | tf_op jit(solution)/shard_map/ppermute | solution.py:207
  30.7 0.8 copy-start.9
  42.7 0.8 copy-start.11
  51.3 1.0 %copy-start.7 = (bf16[512,1024]{1,0:T(8,128)(2,1)}, bf16[512,1024]{1,0:T(8,128)(2,1)S(1)}, u32[]{:S(2)}) copy-start(bf16[512,1024]{1,0:T(8,128)(2,1)S(1)} %collective-permute-done.2.rest_3_) | copy-start | bytes 3145732
  52.3 4.5 %collective-permute-start.7 = (bf16[512,1024]{1,0:T(8,128)(2,1)}, bf16[512,1024]{1,0:T(8,128)(2,1)}, u32[]{:S(2)}, u32[]{:S(2)}) collective-permute-start(bf16[512,1024]{1,0:T(8,128)(2,1)} %collective-permute-done.rest_1_), channel_id=1, source_target_pairs={{0,4},{4,0},{8,12},{12,8},{16,20},{20,16},{24,28},{28,24},{1,5},{5... | collective-permute-start | bytes 3145736 | tf_op jit(solution)/shard_map/ppermute | solution.py:162
  52.3 4.5 %collective-permute-start.8 = (bf16[512,1024]{1,0:T(8,128)(2,1)S(1)}, bf16[512,1024]{1,0:T(8,128)(2,1)}, u32[]{:S(2)}, u32[]{:S(2)}) collective-permute-start(bf16[512,1024]{1,0:T(8,128)(2,1)S(1)} %collective-permute-done.1.rest_2_), channel_id=1, source_target_pairs={{0,4},{4,0},{8,12},{12,8},{16,20},{20,16},{24,28},{28,24},{1,5},{5... | collective-permute-start | bytes 3145736 | tf_op jit(solution)/shard_map/ppermute | solution.py:162
  52.8 25.1 %collective-permute-start.6 = (bf16[512,1024]{1,0:T(8,128)(2,1)S(1)}, bf16[512,1024]{1,0:T(8,128)(2,1)S(1)}, u32[]{:S(2)}, u32[]{:S(2)}) collective-permute-start(bf16[512,1024]{1,0:T(8,128)(2,1)S(1)} %collective-permute-done.1.rest_2_), channel_id=1, source_target_pairs={{0,8},{4,12},{8,0},{12,4},{16,24},{20,28},{24,16},{28,20},{1,9},{5... | collective-permute-start | bytes 3145736 | tf_op jit(solution)/shard_map/ppermute | solution.py:158
  56.7 1.5 %copy-start.1 = (bf16[4,14,128,128]{3,2,1,0:T(8,128)(2,1)S(1)}, bf16[4,14,128,128]{3,2,1,0:T(8,128)(2,1)}, u32[]{:S(2)}) copy-start(bf16[4,14,128,128]{3,2,1,0:T(8,128)(2,1)} %h_ref.4) | copy-start | bytes 5505028
  58.2 3.7 %copy-start.5 = (bf16[8,14,128,128]{3,2,1,0:T(8,128)(2,1)S(1)}, bf16[8,14,128,128]{3,2,1,0:T(8,128)(2,1)}, u32[]{:S(2)}) copy-start(bf16[8,14,128,128]{3,2,1,0:T(8,128)(2,1)} %h_ref.2) | copy-start | bytes 11010052
  59.7 1.5 %copy-start.2 = (bf16[4,14,128,128]{3,2,1,0:T(8,128)(2,1)S(1)}, bf16[4,14,128,128]{3,2,1,0:T(8,128)(2,1)}, u32[]{:S(2)}) copy-start(bf16[4,14,128,128]{3,2,1,0:T(8,128)(2,1)} %h_ref.4) | copy-start | bytes 5505028
  59.7 2.2 %copy-start.4 = (bf16[512,1024]{1,0:T(8,128)(2,1)S(1)}, bf16[512,1024]{1,0:T(8,128)(2,1)}, u32[]{:S(2)}) copy-start(bf16[512,1024]{1,0:T(8,128)(2,1)} %rest_0_) | copy-start | bytes 3145732
  59.7 2.2 %copy-start.10 = (bf16[512,512]{1,0:T(8,128)(2,1)S(1)}, bf16[512,512]{1,0:T(8,128)(2,1)}, u32[]{:S(2)}) copy-start(bf16[512,512]{1,0:T(8,128)(2,1)} %copy-done.9) | copy-start | bytes 1572868
  59.8 2.2 %copy-start.12 = (bf16[512,512]{1,0:T(8,128)(2,1)S(1)}, bf16[512,512]{1,0:T(8,128)(2,1)}, u32[]{:S(2)}) copy-start(bf16[512,512]{1,0:T(8,128)(2,1)} %copy-done.11) | copy-start | bytes 1572868
  61.9 1.6 %copy-start.6 = (f32[512,1024]{1,0:T(8,128)S(1)}, f32[512,1024]{1,0:T(8,128)}, u32[]{:S(2)}) copy-start(f32[512,1024]{1,0:T(8,128)} %d_ref.1) | copy-start | bytes 6291460
  63.5 3.8 %copy-start.8 = (bf16[512,1024]{1,0:T(8,128)(2,1)S(1)}, bf16[512,1024]{1,0:T(8,128)(2,1)}, u32[]{:S(2)}) copy-start(bf16[512,1024]{1,0:T(8,128)(2,1)} %copy-done.7) | copy-start | bytes 3145732
  77.8 2.7 %collective-permute-start.9 = (bf16[512,1024]{1,0:T(8,128)(2,1)S(1)}, bf16[512,1024]{1,0:T(8,128)(2,1)S(1)}, u32[]{:S(2)}, u32[]{:S(2)}) collective-permute-start(bf16[512,1024]{1,0:T(8,128)(2,1)S(1)} %collective-permute-done.6.rest_0_), channel_id=1, source_target_pairs={{0,4},{4,0},{8,12},{12,8},{16,20},{20,16},{24,28},{28,24},{1,5},{5... | collective-permute-start | bytes 3145736 | tf_op jit(solution)/shard_map/ppermute | solution.py:162

commit v3 on v2

--- a/solution.py
+++ b/solution.py
@@ -10,6 +10,7 @@
 
 CAP_B = 4
 CORES = 2
+FIRST = 1
 VMEM_LIMIT = 40 * 1024 * 1024
 
 
@@ -25,26 +26,10 @@
     match = match.reshape(owners, owners, per_owner, CAP_B)
     local = jnp.arange(per_owner, dtype=jnp.int32)[:, None]
     chosen = jnp.max(jnp.where(match, local, -1), axis=2)
-    steps = np.arange(1, owners)
     pack = lax.dynamic_index_in_dim(chosen, me, 1, keepdims=False)
-    pack = jnp.take(pack, partner(me, steps, owners), axis=0)
     got = lax.dynamic_index_in_dim(chosen, me, 0, keepdims=False)
     got = jnp.where(got >= 0, got + jnp.arange(owners, dtype=jnp.int32)[:, None] * per_owner, -1)
-    got = jnp.take(got, partner_back(me, steps, owners), axis=0).reshape(-1)
-    got = jnp.concatenate([me * per_owner + jnp.arange(per_owner, dtype=jnp.int32), got])
-    return jnp.maximum(pack, 0).reshape(-1), got
-
-
-def partner(me, step, owners):
-    if owners & (owners - 1) == 0:
-        return me ^ step
-    return (me + step) % owners
-
-
-def partner_back(me, step, owners):
-    if owners & (owners - 1) == 0:
-        return me ^ step
-    return (me + owners - step) % owners
+    return jnp.maximum(pack, 0).reshape(-1), got.reshape(-1)
 
 
 def slot_table(lists, position_ids):
@@ -53,26 +38,25 @@
     return jnp.max(jnp.where(hit, slots, -1), axis=1)
 
 
-def pack_beta_body(block, pack_ref, c_ref, *outs):
-    for s, out in enumerate(outs):
-        for c in range(CAP_B):
-            j = pack_ref[s * CAP_B + c]
-            column = pl.ds(pl.multiple_of(j * block, block), block)
-            out[:, c * block : (c + 1) * block] = c_ref[:, column]
-
-
 def pack_beta(pack, coefficients, parts, block):
     height = coefficients.shape[0]
-    shape = jax.ShapeDtypeStruct((height, CAP_B * block), coefficients.dtype)
-    return pl.pallas_call(
-        functools.partial(pack_beta_body, block),
+
+    def body(pack_ref, c_ref, out_ref):
+        for s in range(parts):
+            for c in range(CAP_B):
+                j = pack_ref[s * CAP_B + c]
+                column = pl.ds(pl.multiple_of(j * block, block), block)
+                out_ref[s, :, c * block : (c + 1) * block] = c_ref[:, column]
+
+    return pl.pallas_call(
+        body,
         grid_spec=pltpu.PrefetchScalarGridSpec(
             num_scalar_prefetch=1,
             grid=(),
             in_specs=[pl.BlockSpec(memory_space=pltpu.VMEM)],
-            out_specs=[pl.BlockSpec(memory_space=pltpu.VMEM)] * parts,
+            out_specs=pl.BlockSpec(memory_space=pltpu.VMEM),
         ),
-        out_shape=[shape] * parts,
+        out_shape=jax.ShapeDtypeStruct((parts, height, CAP_B * block), coefficients.dtype),
         compiler_params=pltpu.CompilerParams(vmem_limit_bytes=VMEM_LIMIT),
         name="pack_beta",
     )(pack, coefficients)
@@ -88,33 +72,31 @@
             )
 
 
-def beta_body(rows, positions, block, table_ref, h_ref, d_ref, c_ref, *rest):
-    arrived, out_ref, weights = rest[:-2], rest[-2], rest[-1]
-    fill(weights, table_ref, h_ref, rows, positions, block)
-    own = c_ref[...]
-    x = jnp.concatenate([own] + [a[...] for a in arrived], axis=1)
-    total = lax.dot_general(
-        x, weights[...], (((1,), (1,)), ((), ())), preferred_element_type=jnp.float32
-    )
-    out_ref[...] = total + d_ref[...] * own.astype(jnp.float32)
-
-
 def beta_product(table, beta_blocks, coefficients, diagonal, arrived):
     rows, block = beta_blocks.shape[0], beta_blocks.shape[2]
-    positions = table.shape[1]
-    return pl.pallas_call(
-        functools.partial(beta_body, rows, positions, block),
+    parts, positions = arrived.shape[0], table.shape[1]
+
+    def body(table_ref, h_ref, d_ref, c_ref, x_ref, out_ref, weights):
+        fill(weights, table_ref, h_ref, rows, positions, block)
+        x = jnp.concatenate([x_ref[s] for s in range(parts)], axis=1)
+        total = lax.dot_general(
+            x, weights[...], (((1,), (1,)), ((), ())), preferred_element_type=jnp.float32
+        )
+        out_ref[...] = total + d_ref[...] * c_ref[...].astype(jnp.float32)
+
+    return pl.pallas_call(
+        body,
         grid_spec=pltpu.PrefetchScalarGridSpec(
             num_scalar_prefetch=1,
             grid=(),
-            in_specs=[pl.BlockSpec(memory_space=pltpu.VMEM)] * (3 + len(arrived)),
+            in_specs=[pl.BlockSpec(memory_space=pltpu.VMEM)] * 4,
             out_specs=pl.BlockSpec(memory_space=pltpu.VMEM),
             scratch_shapes=[pltpu.VMEM((rows * block, positions * block), jnp.bfloat16)],
         ),
         out_shape=jax.ShapeDtypeStruct(diagonal.shape, jnp.float32),
         compiler_params=pltpu.CompilerParams(vmem_limit_bytes=VMEM_LIMIT),
         name="beta_product",
-    )(table.reshape(-1), beta_blocks, diagonal, coefficients, *arrived)
+    )(table.reshape(-1), beta_blocks, diagonal, coefficients, arrived)
 
 
 def lay_out(table, blocks):
@@ -201,11 +183,9 @@
     def beta_all(arrived):
         return beta_product(table_b, beta_blocks, coefficients, diagonal, arrived)
 
-    def exchange(packed):
-        steps = range(1, owners_b)
-        return [
-            lax.ppermute(packed[s - 1], "beta", [(d, partner(d, s, owners_b)) for d in range(owners_b)]) for s in steps
-        ]
+    def exchange():
+        packed = pack_beta(pack, coefficients, owners_b, block)
+        return lax.all_to_all(packed, "beta", split_axis=0, concat_axis=0, tiled=True)
 
     everyone = range(chips)
     own = [place(p, 0, rows_a) for p in everyone]
@@ -214,32 +194,36 @@
         far_from, near_from, both_from = [2, 3, 0, 1], [1, 0, 3, 2], [3, 2, 1, 0]
 
 
-        def of(chip_of):
-            return [place(chip_of[p], 0, rows_a) for p in everyone]
-
-        table_here = table_of([own, of(near_from), of(far_from)])
-        table_both = table_of([of(both_from)])
-        half = table_both.shape[1] // 2
-
-        near_own, far_own = send(coefficients, near), send(coefficients, far)
-        arrived = exchange(pack_beta(pack, coefficients, owners_b - 1, block))
+        cuts = [(0, FIRST), (FIRST, rows_a - FIRST)]
+
+        def of(chip_of, first=0, count=rows_a):
+            return [place(chip_of[p], first, count) for p in everyone]
+
+        table_here = table_of([own, of(near_from)] + [of(far_from, *cut) for cut in cuts] + [of(both_from, *cuts[0])])
+        table_last = table_of([of(both_from, *cuts[1])])
+        half = table_last.shape[1] // 2
+        tables = (table_here, table_last[:, :half], table_last[:, half:])
+
+        far_own = [send(coefficients[f * block : (f + n) * block], far) for f, n in cuts]
+        near_own = send(coefficients, near)
+        near_far = send(far_own[0], near)
         own_swapped = swap(coefficients, everyone)
-        near_own, far_own, own_swapped, here, table_here, table_b, table_same, table_other, *arrived = gate(
-            near_own, far_own, own_swapped, coefficients, table_here, table_b, table_both[:, :half], table_both[:, half:], *arrived
+        arrived = exchange()
+        near_far, near_own, far_own[1], own_swapped, here, table_b, *tables = gate(
+            near_far, near_own, far_own[1], own_swapped, coefficients, table_b, *tables
         )
-
-        near_far = send(far_own, near)
-        pieces = [here, near_own, far_own]
-        pieces += [own_swapped, swap(near_own, everyone), swap(far_own, everyone)]
-        *pieces, here, blocks_here = gate(*pieces, here, alpha_blocks)
+        near_last = send(far_own[1], near)
+        pieces = [here, near_own, *far_own, near_far]
+        pieces += [own_swapped] + [swap(x, everyone) for x in pieces[1:]]
+        *pieces, here, blocks_here, arrived = gate(*pieces, here, alpha_blocks, arrived)
+        weights = [lay_out(table, blocks_here) for table in tables]
         acc = beta_product(table_b, beta_blocks, here, diagonal, arrived)
-        weights = [lay_out(table, blocks_here) for table in (table_here, table_same, table_other)]
         acc = alpha_product(weights[0], pieces, acc, jnp.float32)
-        near_far, acc, *weights = gate(near_far, acc, *weights)
-        acc = alpha_product(weights[1], [near_far], acc, jnp.float32)
-        return alpha_product(weights[2], [swap(near_far, everyone)], acc, jnp.bfloat16)
-
-    arrived = exchange(pack_beta(pack, coefficients, owners_b - 1, block))
+        near_last, acc, *weights = gate(near_last, acc, *weights)
+        acc = alpha_product(weights[1], [near_last], acc, jnp.float32)
+        return alpha_product(weights[2], [swap(near_last, everyone)], acc, jnp.bfloat16)
+
+    arrived = exchange()
     pieces, places = [coefficients], [own]
     left, right = [], []
     for u in range((chips - 1) * rows_a):

time: 82.6 us -> 79.7 us (0.965)
  local copies, waits for them, and re-layouts: 13.6 us -> 7.97 us
  starting transfers between devices: 12 us -> 17.1 us
  waiting for transfers between devices: 38.3 us -> 34.4 us
  Pallas kernels: 16.2 us -> 18.4 us
  other arithmetic: 1.99 us -> 1.16 us
    ppermute x3 -> x0, waiting for transfers between devices: 20.1 us -> none  [exchange(): lax.ppermute(packed[s - 1], 'beta', [(d, partner(d, s, owners_b)) for d i...]
    ppermute x3 -> x5, waiting for transfers between devices: 13 us -> 32.4 us  [send(): lax.ppermute(x, 'alpha', [(s * CORES + c, t * CORES + c) for s, t in edge...]
    unnamed x29 -> x15, local copies, waits for them, and re-layouts: 9.3 us -> 2.18 us
    ppermute x3 -> x0, starting transfers between devices: 5.46 us -> none  [exchange(): lax.ppermute(packed[s - 1], 'beta', [(d, partner(d, s, owners_b)) for d i...]
    ppermute x3 -> x5, starting transfers between devices: 6.04 us -> 11.4 us  [send(): lax.ppermute(x, 'alpha', [(s * CORES + c, t * CORES + c) for s, t in edge...]
    all_to_all x0 -> x1, starting transfers between devices: none -> 4.57 us  [exchange(): lax.all_to_all(packed, 'beta', split_axis=0, concat_axis=0, tiled=True)]
    ppermute x4 -> x6, waiting for transfers between devices: 5.15 us -> 2 us  [swap(): lax.ppermute(x, 'alpha', [(p * CORES + c, p * CORES + 1 - c) for p in chi...]
    slice x1 -> x3, local copies, waits for them, and re-layouts: 0.07 us -> 3.06 us  [the longest x2 3.06 us: per_device(): coefficients[f * block:(f + n) * block]]
  transfers between devices with their start and end apart: 10 -> 12, of which waited for: 7 -> 6; matrix products, arithmetic and copies ran while one was open for 9% -> 9% of each run, Pallas kernels for 18% -> 21%
where the time goes in v3:
time: 79.7 us; the launch traced here: 79.2 us
  waiting for transfers between devices  34.4 us (43%)
  Pallas kernels  18.4 us (23%)
  starting transfers between devices  17.1 us (21%)
  local copies, waits for them, and re-layouts  7.97 us (10%)
  other arithmetic  1.16 us (1%)
    ppermute x5, waiting for transfers between devices, send(): lax.ppermute(x, 'alpha', [(s * CORES + c, t * CORES + c) for s, t in edge...  32.4 us
    ppermute x5, starting transfers between devices, send(): lax.ppermute(x, 'alpha', [(s * CORES + c, t * CORES + c) for s, t in edge...  11.4 us
    pallas_call x3, Pallas kernels, alpha_product(): pl.pallas_call(body, in_specs=[pl.BlockSpec(memory_space=pltpu.VMEM)] * (...  9.7 us
    pallas_call x1, Pallas kernels, beta_product(): pl.pallas_call(body, grid_spec=pltpu.PrefetchScalarGridSpec(num_scalar_pr...  4.93 us
    all_to_all x1, starting transfers between devices, exchange(): lax.all_to_all(packed, 'beta', split_axis=0, concat_axis=0, tiled=True)  4.57 us
    slice x2, local copies, waits for them, and re-layouts, per_device(): coefficients[f * block:(f + n) * block]  3.06 us
    pallas_call x3, Pallas kernels, lay_out(): pl.pallas_call(body, grid_spec=pltpu.PrefetchScalarGridSpec(num_scalar_pr...  2.65 us
    unnamed x15, local copies, waits for them, and re-layouts  2.18 us
  transfers between devices with their start and end apart: 12, of which 6 were waited for; matrix products, arithmetic and copies ran while one was open for 9% of the time, Pallas kernels for 21%

profile of v3, /device:TPU:0, one launch (start us, length us, event | category | flops | bytes accessed | tf_op | source)
XLA Modules:
  0.0 79.2 jit_solution(12463876377921142612)
XLA Ops:
  0.0 3.1 %collective-permute-start.2 = (bf16[512,1024]{1,0:T(8,128)(2,1)}, bf16[512,1024]{1,0:T(8,128)(2,1)}, u32[]{:S(2)}, u32[]{:S(2)}) collective-permute-start(bf16[512,1024]{1,0:T(8,128)(2,1)} %rest_0_), channel_id=1, source_target_pairs={{0,8},{4,12},{8,0},{12,4},{16,24},{20,28},{24,16},{28,20},{1,9},{5... | collective-permute-start | bytes 3145736 | tf_op jit(solution)/shard_map/ppermute | solution.py:140
  3.1 1.0 %slice.12 = bf16[128,1024]{1,0:T(8,128)(2,1)S(1)} slice(bf16[512,1024]{1,0:T(8,128)(2,1)} %rest_0_), slice={[0:128], [0:1024]} | slice | bytes 524288 | tf_op jit(solution)/shard_map/slice | solution.py:207
  4.1 2.7 %collective-permute-start = (bf16[128,1024]{1,0:T(8,128)(2,1)S(1)}, bf16[128,1024]{1,0:T(8,128)(2,1)S(1)}, u32[]{:S(2)}, u32[]{:S(2)}) collective-permute-start(bf16[128,1024]{1,0:T(8,128)(2,1)S(1)} %slice.12), channel_id=1, source_target_pairs={{0,16},{4,20},{8,24},{12,28},{16,0},{20,4},{24,8},{28,12},{1,17},{... | collective-permute-start | bytes 786440 | tf_op jit(solution)/shard_map/ppermute | solution.py:140
  6.8 2.1 %slice.13 = bf16[384,1024]{1,0:T(8,128)(2,1)} slice(bf16[512,1024]{1,0:T(8,128)(2,1)} %rest_0_), slice={[128:512], [0:1024]} | slice | bytes 1572864 | tf_op jit(solution)/shard_map/slice | solution.py:207
  10.3 1.1 %pack_beta.1 = bf16[4,512,512]{2,1,0:T(8,128)(2,1)S(1)} custom-call(s32[16]{0:T(128)S(1)} %max.8.pack_ref, bf16[512,1024]{1,0:T(8,128)(2,1)S(1)} %copy-done.1), custom_call_target="tpu_custom_call" | custom-call | tf_op jit(solution)/shard_map/pack_beta/pallas_call | solution.py:51
  11.4 1.3 %copy-done.3 = bf16[4,512,512]{2,1,0:T(8,128)(2,1)} copy-done((bf16[4,512,512]{2,1,0:T(8,128)(2,1)}, bf16[4,512,512]{2,1,0:T(8,128)(2,1)S(1)}, u32[]{:S(2)}) %copy-start.3) | copy-done | bytes 2097176
  12.7 4.6 %all-to-all-start = ((bf16[4,512,512]{2,1,0:T(8,128)(2,1)}), bf16[4,512,512]{2,1,0:T(8,128)(2,1)}, u32[]{:S(2)}, u32[]{:S(2)}) async-start(bf16[4,512,512]{2,1,0:T(8,128)(2,1)} %copy-done.3), calls=%async_computation | async-start | bytes 4194304 | tf_op jit(solution)/shard_map/all_to_all | solution.py:188
  17.4 0.7 fusion.3
  18.6 0.7 fusion.4
  19.4 13.1 %collective-permute-done.rest_2_ = bf16[128,1024]{1,0:T(8,128)(2,1)S(1)} collective-permute-done((bf16[128,1024]{1,0:T(8,128)(2,1)S(1)}, bf16[128,1024]{1,0:T(8,128)(2,1)S(1)}, u32[]{:S(2)}, u32[]{:S(2)}) %collective-permute-start) | collective-permute-done | bytes 262176 | tf_op jit(solution)/shard_map/ppermute | solution.py:140
  32.5 3.5 %collective-permute-start.1 = (bf16[128,1024]{1,0:T(8,128)(2,1)S(1)}, bf16[128,1024]{1,0:T(8,128)(2,1)S(1)}, u32[]{:S(2)}, u32[]{:S(2)}) collective-permute-start(bf16[128,1024]{1,0:T(8,128)(2,1)S(1)} %collective-permute-done.rest_2_), channel_id=1, source_target_pairs={{0,8},{4,12},{8,0},{12,4},{16,24},{20,28},{24,16},{28,20},{1,9},{5... | collective-permute-start | bytes 786440 | tf_op jit(solution)/shard_map/ppermute | solution.py:140
  36.3 18.2 %collective-permute-done.1.rest_4_ = bf16[128,1024]{1,0:T(8,128)(2,1)S(1)} collective-permute-done((bf16[128,1024]{1,0:T(8,128)(2,1)S(1)}, bf16[128,1024]{1,0:T(8,128)(2,1)S(1)}, u32[]{:S(2)}, u32[]{:S(2)}) %collective-permute-start.1) | collective-permute-done | bytes 262176 | tf_op jit(solution)/shard_map/ppermute | solution.py:140
  55.1 1.8 %collective-permute-start.5 = (bf16[384,1024]{1,0:T(8,128)(2,1)}, bf16[384,1024]{1,0:T(8,128)(2,1)}, u32[]{:S(2)}, u32[]{:S(2)}) collective-permute-start(bf16[384,1024]{1,0:T(8,128)(2,1)} %collective-permute-done.3.rest_3_), channel_id=1, source_target_pairs={{0,8},{4,12},{8,0},{12,4},{16,24},{20,28},{24,16},{28,20},{1,9},{5... | collective-permute-start | bytes 2359304 | tf_op jit(solution)/shard_map/ppermute | solution.py:140
  58.0 1.0 %collective-permute-done.7.rest_7_ = bf16[128,1024]{1,0:T(8,128)(2,1)} collective-permute-done((bf16[128,1024]{1,0:T(8,128)(2,1)S(1)}, bf16[128,1024]{1,0:T(8,128)(2,1)}, u32[]{:S(2)}, u32[]{:S(2)}) %collective-permute-start.7) | collective-permute-done | bytes 262176 | tf_op jit(solution)/shard_map/ppermute | solution.py:144
  59.3 1.4 %lay_out.3.w_ref = bf16[512,3328]{1,0:T(8,128)(2,1)S(1)} custom-call(s32[104]{0:T(128)S(1)} %reshape.165.table_ref, bf16[4,14,128,128]{3,2,1,0:T(8,128)(2,1)S(1)} %copy-done.2), custom_call_target="tpu_custom_call" | custom-call | tf_op jit(solution)/shard_map/lay_out/pallas_call | solution.py:109
  60.7 0.6 lay_out.4.w_ref
  61.4 0.6 lay_out.5.w_ref
  62.0 0.8 copy-done.4
  62.8 4.9 %beta_product.1.acc_ref = f32[512,1024]{1,0:T(8,128)S(1)} custom-call(s32[128]{0:T(128)S(1)} %reshape.166.table_ref, bf16[8,14,128,128]{3,2,1,0:T(8,128)(2,1)S(1)} %copy-done.4, f32[512,1024]{1,0:T(8,128)S(1)} %copy-done.5, bf16[512,1024]{1,0:T(8,128)(2,1)S(1)} %copy-done.1, bf16[4,512,512]{2,1,0:T(8,128)(2,1)} %all-to-all-done.x_ref), custom_call_target="tpu_custom_call" | custom-call | tf_op jit(solution)/shard_map/beta_product/pallas_call | solution.py:87
  67.7 6.2 %alpha_product.3.acc_ref = f32[512,1024]{1,0:T(8,128)S(1)} custom-call(bf16[512,3328]{1,0:T(8,128)(2,1)S(1)} %lay_out.3.w_ref, f32[512,1024]{1,0:T(8,128)S(1)} %beta_product.1.acc_ref, bf16[512,1024]{1,0:T(8,128)(2,1)S(1)} %copy-done.1, bf16[512,1024]{1,0:T(8,128)(2,1)} %collective-permute-done.2.rest_1_, ...), custom_call_target="tpu_custom_call" | custom-call | tf_op jit(solution)/shard_map/alpha_product/pallas_call | solution.py:129
  73.9 1.1 %collective-permute-done.5.rest_0_ = bf16[384,1024]{1,0:T(8,128)(2,1)} collective-permute-done((bf16[384,1024]{1,0:T(8,128)(2,1)}, bf16[384,1024]{1,0:T(8,128)(2,1)}, u32[]{:S(2)}, u32[]{:S(2)}) %collective-permute-start.5) | collective-permute-done | bytes 786464 | tf_op jit(solution)/shard_map/ppermute | solution.py:140
  75.0 1.8 %alpha_product.4.acc_ref = f32[512,1024]{1,0:T(8,128)S(1)} custom-call(bf16[512,384]{1,0:T(8,128)(2,1)S(1)} %lay_out.4.w_ref, f32[512,1024]{1,0:T(8,128)S(1)} %alpha_product.3.acc_ref, bf16[384,1024]{1,0:T(8,128)(2,1)} %collective-permute-done.5.rest_0_), custom_call_target="tpu_custom_call" | custom-call | tf_op jit(solution)/shard_map/alpha_product/pallas_call | solution.py:129
  76.9 0.6 collective-permute-done.10.rest_0_
  77.5 1.7 %alpha_product.5 = bf16[512,1024]{1,0:T(8,128)(2,1)} custom-call(bf16[512,384]{1,0:T(8,128)(2,1)S(1)} %lay_out.5.w_ref, f32[512,1024]{1,0:T(8,128)S(1)} %alpha_product.4.acc_ref, bf16[384,1024]{1,0:T(8,128)(2,1)S(1)} %collective-permute-done.10.rest_0_), custom_call_target="tpu_custom_call" | custom-call | tf_op jit(solution)/shard_map/alpha_product/pallas_call | solution.py:129
  (56 shorter events, 4.4 us)
Async XLA Ops:
  0.0 17.3 %copy-start = (s32[32,14]{0,1:T(8,128)S(1)}, s32[32,14]{0,1:T(8,128)}, u32[]{:S(2)}) copy-start(s32[32,14]{0,1:T(8,128)} %param.11) | copy-start | bytes 5380
  0.0 10.3 %copy-start.1 = (bf16[512,1024]{1,0:T(8,128)(2,1)S(1)}, bf16[512,1024]{1,0:T(8,128)(2,1)}, u32[]{:S(2)}) copy-start(bf16[512,1024]{1,0:T(8,128)(2,1)} %rest_0_) | copy-start | bytes 3145732
  0.0 9.2 %copy-start.6 = (s32[32,14]{0,1:T(8,128)S(1)}, s32[32,14]{0,1:T(8,128)}, u32[]{:S(2)}) copy-start(s32[32,14]{0,1:T(8,128)} %param.13) | copy-start | bytes 5380
  0.0 54.6 %collective-permute-start.2 = (bf16[512,1024]{1,0:T(8,128)(2,1)}, bf16[512,1024]{1,0:T(8,128)(2,1)}, u32[]{:S(2)}, u32[]{:S(2)}) collective-permute-start(bf16[512,1024]{1,0:T(8,128)(2,1)} %rest_0_), channel_id=1, source_target_pairs={{0,8},{4,12},{8,0},{12,4},{16,24},{20,28},{24,16},{28,20},{1,9},{5... | collective-permute-start | bytes 3145736 | tf_op jit(solution)/shard_map/ppermute | solution.py:140
  3.1 51.5 %collective-permute-start.4 = (bf16[512,1024]{1,0:T(8,128)(2,1)}, bf16[512,1024]{1,0:T(8,128)(2,1)}, u32[]{:S(2)}, u32[]{:S(2)}) collective-permute-start(bf16[512,1024]{1,0:T(8,128)(2,1)} %rest_0_), channel_id=1, source_target_pairs={{0,4},{4,0},{8,12},{12,8},{16,20},{20,16},{24,28},{28,24},{1,5},{5... | collective-permute-start | bytes 3145736 | tf_op jit(solution)/shard_map/ppermute | solution.py:144
  4.1 28.4 %collective-permute-start = (bf16[128,1024]{1,0:T(8,128)(2,1)S(1)}, bf16[128,1024]{1,0:T(8,128)(2,1)S(1)}, u32[]{:S(2)}, u32[]{:S(2)}) collective-permute-start(bf16[128,1024]{1,0:T(8,128)(2,1)S(1)} %slice.12), channel_id=1, source_target_pairs={{0,16},{4,20},{8,24},{12,28},{16,0},{20,4},{24,8},{28,12},{1,17},{... | collective-permute-start | bytes 786440 | tf_op jit(solution)/shard_map/ppermute | solution.py:140
  8.8 45.7 %collective-permute-start.3 = (bf16[384,1024]{1,0:T(8,128)(2,1)}, bf16[384,1024]{1,0:T(8,128)(2,1)}, u32[]{:S(2)}, u32[]{:S(2)}) collective-permute-start(bf16[384,1024]{1,0:T(8,128)(2,1)} %slice.13), channel_id=1, source_target_pairs={{0,16},{4,20},{8,24},{12,28},{16,0},{20,4},{24,8},{28,12},{1,17},{... | collective-permute-start | bytes 2359304 | tf_op jit(solution)/shard_map/ppermute | solution.py:140
  11.4 1.3 %copy-start.3 = (bf16[4,512,512]{2,1,0:T(8,128)(2,1)}, bf16[4,512,512]{2,1,0:T(8,128)(2,1)S(1)}, u32[]{:S(2)}) copy-start(bf16[4,512,512]{2,1,0:T(8,128)(2,1)S(1)} %pack_beta.1) | copy-start | bytes 6291460
  12.7 46.6 %copy-start.2 = (bf16[4,14,128,128]{3,2,1,0:T(8,128)(2,1)S(1)}, bf16[4,14,128,128]{3,2,1,0:T(8,128)(2,1)}, u32[]{:S(2)}) copy-start(bf16[4,14,128,128]{3,2,1,0:T(8,128)(2,1)} %h_ref.4) | copy-start | bytes 5505028
  12.7 46.6 %all-to-all-start = ((bf16[4,512,512]{2,1,0:T(8,128)(2,1)}), bf16[4,512,512]{2,1,0:T(8,128)(2,1)}, u32[]{:S(2)}, u32[]{:S(2)}) async-start(bf16[4,512,512]{2,1,0:T(8,128)(2,1)} %copy-done.3), calls=%async_computation | async-start | bytes 4194304 | tf_op jit(solution)/shard_map/all_to_all | solution.py:188
  32.5 22.0 %collective-permute-start.1 = (bf16[128,1024]{1,0:T(8,128)(2,1)S(1)}, bf16[128,1024]{1,0:T(8,128)(2,1)S(1)}, u32[]{:S(2)}, u32[]{:S(2)}) collective-permute-start(bf16[128,1024]{1,0:T(8,128)(2,1)S(1)} %collective-permute-done.rest_2_), channel_id=1, source_target_pairs={{0,8},{4,12},{8,0},{12,4},{16,24},{20,28},{24,16},{28,20},{1,9},{5... | collective-permute-start | bytes 786440 | tf_op jit(solution)/shard_map/ppermute | solution.py:140
  54.6 4.7 %collective-permute-start.6 = (bf16[512,1024]{1,0:T(8,128)(2,1)}, bf16[512,1024]{1,0:T(8,128)(2,1)}, u32[]{:S(2)}, u32[]{:S(2)}) collective-permute-start(bf16[512,1024]{1,0:T(8,128)(2,1)} %collective-permute-done.2.rest_1_), channel_id=1, source_target_pairs={{0,4},{4,0},{8,12},{12,8},{16,20},{20,16},{24,28},{28,24},{1,5},{5... | collective-permute-start | bytes 3145736 | tf_op jit(solution)/shard_map/ppermute | solution.py:144
  54.7 4.7 %collective-permute-start.8 = (bf16[384,1024]{1,0:T(8,128)(2,1)}, bf16[384,1024]{1,0:T(8,128)(2,1)}, u32[]{:S(2)}, u32[]{:S(2)}) collective-permute-start(bf16[384,1024]{1,0:T(8,128)(2,1)} %collective-permute-done.3.rest_3_), channel_id=1, source_target_pairs={{0,4},{4,0},{8,12},{12,8},{16,20},{20,16},{24,28},{28,24},{1,5},{5... | collective-permute-start | bytes 2359304 | tf_op jit(solution)/shard_map/ppermute | solution.py:144
  55.1 19.9 %collective-permute-start.5 = (bf16[384,1024]{1,0:T(8,128)(2,1)}, bf16[384,1024]{1,0:T(8,128)(2,1)}, u32[]{:S(2)}, u32[]{:S(2)}) collective-permute-start(bf16[384,1024]{1,0:T(8,128)(2,1)} %collective-permute-done.3.rest_3_), channel_id=1, source_target_pairs={{0,8},{4,12},{8,0},{12,4},{16,24},{20,28},{24,16},{28,20},{1,9},{5... | collective-permute-start | bytes 2359304 | tf_op jit(solution)/shard_map/ppermute | solution.py:140
  56.9 2.0 %collective-permute-start.7 = (bf16[128,1024]{1,0:T(8,128)(2,1)S(1)}, bf16[128,1024]{1,0:T(8,128)(2,1)}, u32[]{:S(2)}, u32[]{:S(2)}) collective-permute-start(bf16[128,1024]{1,0:T(8,128)(2,1)S(1)} %collective-permute-done.rest_2_), channel_id=1, source_target_pairs={{0,4},{4,0},{8,12},{12,8},{16,20},{20,16},{24,28},{28,24},{1,5},{5... | collective-permute-start | bytes 786440 | tf_op jit(solution)/shard_map/ppermute | solution.py:144
  56.9 2.4 %collective-permute-start.9 = (bf16[128,1024]{1,0:T(8,128)(2,1)S(1)}, bf16[128,1024]{1,0:T(8,128)(2,1)}, u32[]{:S(2)}, u32[]{:S(2)}) collective-permute-start(bf16[128,1024]{1,0:T(8,128)(2,1)S(1)} %collective-permute-done.1.rest_4_), channel_id=1, source_target_pairs={{0,4},{4,0},{8,12},{12,8},{16,20},{20,16},{24,28},{28,24},{1,5},{5... | collective-permute-start | bytes 786440 | tf_op jit(solution)/shard_map/ppermute | solution.py:144
  59.3 2.7 %copy-start.5 = (f32[512,1024]{1,0:T(8,128)S(1)}, f32[512,1024]{1,0:T(8,128)}, u32[]{:S(2)}) copy-start(f32[512,1024]{1,0:T(8,128)} %d_ref.1) | copy-start | bytes 6291460
  60.7 2.1 %copy-start.4 = (bf16[8,14,128,128]{3,2,1,0:T(8,128)(2,1)S(1)}, bf16[8,14,128,128]{3,2,1,0:T(8,128)(2,1)}, u32[]{:S(2)}) copy-start(bf16[8,14,128,128]{3,2,1,0:T(8,128)(2,1)} %h_ref.2) | copy-start | bytes 11010052
  75.0 2.5 %collective-permute-start.10 = (bf16[384,1024]{1,0:T(8,128)(2,1)}, bf16[384,1024]{1,0:T(8,128)(2,1)S(1)}, u32[]{:S(2)}, u32[]{:S(2)}) collective-permute-start(bf16[384,1024]{1,0:T(8,128)(2,1)} %collective-permute-done.5.rest_0_), channel_id=1, source_target_pairs={{0,4},{4,0},{8,12},{12,8},{16,20},{20,16},{24,28},{28,24},{1,5},{5... | collective-permute-start | bytes 2359304 | tf_op jit(solution)/shard_map/ppermute | solution.py:144

commit v4 on v3

--- a/solution.py
+++ b/solution.py
@@ -72,31 +72,31 @@
             )
 
 
-def beta_product(table, beta_blocks, coefficients, diagonal, arrived):
+def beta_product(table, beta_blocks, coefficients, diagonal, arrived, acc):
     rows, block = beta_blocks.shape[0], beta_blocks.shape[2]
     parts, positions = arrived.shape[0], table.shape[1]
 
-    def body(table_ref, h_ref, d_ref, c_ref, x_ref, out_ref, weights):
+    def body(table_ref, h_ref, d_ref, c_ref, x_ref, acc_ref, out_ref, weights):
         fill(weights, table_ref, h_ref, rows, positions, block)
         x = jnp.concatenate([x_ref[s] for s in range(parts)], axis=1)
         total = lax.dot_general(
             x, weights[...], (((1,), (1,)), ((), ())), preferred_element_type=jnp.float32
         )
-        out_ref[...] = total + d_ref[...] * c_ref[...].astype(jnp.float32)
+        out_ref[...] = acc_ref[...] + total + d_ref[...] * c_ref[...].astype(jnp.float32)
 
     return pl.pallas_call(
         body,
         grid_spec=pltpu.PrefetchScalarGridSpec(
             num_scalar_prefetch=1,
             grid=(),
-            in_specs=[pl.BlockSpec(memory_space=pltpu.VMEM)] * 4,
+            in_specs=[pl.BlockSpec(memory_space=pltpu.VMEM)] * 5,
             out_specs=pl.BlockSpec(memory_space=pltpu.VMEM),
             scratch_shapes=[pltpu.VMEM((rows * block, positions * block), jnp.bfloat16)],
         ),
         out_shape=jax.ShapeDtypeStruct(diagonal.shape, jnp.float32),
         compiler_params=pltpu.CompilerParams(vmem_limit_bytes=VMEM_LIMIT),
         name="beta_product",
-    )(table.reshape(-1), beta_blocks, diagonal, coefficients, arrived)
+    )(table.reshape(-1), beta_blocks, diagonal, coefficients, arrived, acc)
 
 
 def lay_out(table, blocks):
@@ -121,19 +121,23 @@
 
 
 def alpha_product(weights, pieces, acc, dtype):
-    def body(w_ref, acc_ref, *rest):
-        x = jnp.concatenate([p[...] for p in rest[:-1]], axis=0)
-        total = acc_ref[...] + jnp.dot(w_ref[...], x, preferred_element_type=jnp.float32)
+    adds = [] if acc is None else [acc]
+
+    def body(w_ref, *rest):
+        x = jnp.concatenate([p[...] for p in rest[len(adds) : -1]], axis=0)
+        total = jnp.dot(w_ref[...], x, preferred_element_type=jnp.float32)
+        if adds:
+            total = rest[0][...] + total
         rest[-1][...] = total.astype(dtype)
 
     return pl.pallas_call(
         body,
-        in_specs=[pl.BlockSpec(memory_space=pltpu.VMEM)] * (2 + len(pieces)),
+        in_specs=[pl.BlockSpec(memory_space=pltpu.VMEM)] * (1 + len(adds) + len(pieces)),
         out_specs=pl.BlockSpec(memory_space=pltpu.VMEM),
-        out_shape=jax.ShapeDtypeStruct(acc.shape, dtype),
+        out_shape=jax.ShapeDtypeStruct((weights.shape[0], pieces[0].shape[1]), dtype),
         compiler_params=pltpu.CompilerParams(vmem_limit_bytes=VMEM_LIMIT),
         name="alpha_product",
-    )(weights, acc, *pieces)
+    )(weights, *adds, *pieces)
 
 
 def send(x, edges):
@@ -180,9 +184,6 @@
 
     table_b = slot_table(mine_b, beta_ids)
 
-    def beta_all(arrived):
-        return beta_product(table_b, beta_blocks, coefficients, diagonal, arrived)
-
     def exchange():
         packed = pack_beta(pack, coefficients, owners_b, block)
         return lax.all_to_all(packed, "beta", split_axis=0, concat_axis=0, tiled=True)
@@ -209,17 +210,15 @@
         near_far = send(far_own[0], near)
         own_swapped = swap(coefficients, everyone)
         arrived = exchange()
-        near_far, near_own, far_own[1], own_swapped, here, table_b, *tables = gate(
-            near_far, near_own, far_own[1], own_swapped, coefficients, table_b, *tables
-        )
+        weights = [lay_out(table, alpha_blocks) for table in tables]
+        near_far, far_own[1], here, table_b, *weights = gate(near_far, far_own[1], coefficients, table_b, *weights)
         near_last = send(far_own[1], near)
         pieces = [here, near_own, *far_own, near_far]
         pieces += [own_swapped] + [swap(x, everyone) for x in pieces[1:]]
-        *pieces, here, blocks_here, arrived = gate(*pieces, here, alpha_blocks, arrived)
-        weights = [lay_out(table, blocks_here) for table in tables]
-        acc = beta_product(table_b, beta_blocks, here, diagonal, arrived)
-        acc = alpha_product(weights[0], pieces, acc, jnp.float32)
-        near_last, acc, *weights = gate(near_last, acc, *weights)
+        *pieces, here, arrived = gate(*pieces, here, arrived)
+        acc = alpha_product(weights[0], pieces, None, jnp.float32)
+        acc = beta_product(table_b, beta_blocks, here, diagonal, arrived, acc)
+        near_last, acc = gate(near_last, acc)
         acc = alpha_product(weights[1], [near_last], acc, jnp.float32)
         return alpha_product(weights[2], [swap(near_last, everyone)], acc, jnp.bfloat16)
 
@@ -233,7 +232,8 @@
         right.append(send(mine if u < rows_a else right[u - rows_a], [(p, p + 1) for p in range(chips - 1) if kind < p + 1]))
         pieces += [left[u], right[u]]
         places += [[place(p + 1 + kind, v, 1) for p in everyone], [place(p - 1 - kind, v, 1) for p in everyone]]
-    acc = beta_product(table_b, beta_blocks, coefficients, diagonal, arrived)
+    acc = jnp.zeros(diagonal.shape, jnp.float32)
+    acc = beta_product(table_b, beta_blocks, coefficients, diagonal, arrived, acc)
     step = 2 * rows_a
     for k in range(0, len(pieces), step):
         last = k + step >= len(pieces)

time: 79.7 us -> 79.3 us (level)
  local copies, waits for them, and re-layouts: 7.97 us -> 12.4 us
  waiting for transfers between devices: 34.4 us -> 30.9 us
  Pallas kernels: 18.4 us -> 17.3 us
    ppermute x5, waiting for transfers between devices: 32.4 us -> 26.4 us  [send(): lax.ppermute(x, 'alpha', [(s * CORES + c, t * CORES + c) for s, t in edge...]
    unnamed x15 -> x25, local copies, waits for them, and re-layouts: 2.18 us -> 5.88 us
    ppermute x6, waiting for transfers between devices: 2 us -> 4.45 us  [swap(): lax.ppermute(x, 'alpha', [(p * CORES + c, p * CORES + 1 - c) for p in chi...]
    pallas_call x3, Pallas kernels: 9.7 us -> 8.47 us  [alpha_product(): pl.pallas_call(body, in_specs=[pl.BlockSpec(memory_space=pltpu.VMEM)] * (...]
  transfers between devices with their start and end apart: 12 -> 12, of which waited for: 6 -> 7; matrix products, arithmetic and copies ran while one was open for 9% -> 10% of each run, Pallas kernels for 21% -> 20%
where the time goes in v4:
time: 79.3 us; the launch traced here: 78.9 us
  waiting for transfers between devices  30.9 us (39%)
  Pallas kernels  17.3 us (22%)
  starting transfers between devices  16.4 us (21%)
  local copies, waits for them, and re-layouts  12.4 us (16%)
  other arithmetic  1.66 us (2%)
    ppermute x5, waiting for transfers between devices, send(): lax.ppermute(x, 'alpha', [(s * CORES + c, t * CORES + c) for s, t in edge...  26.4 us
    ppermute x5, starting transfers between devices, send(): lax.ppermute(x, 'alpha', [(s * CORES + c, t * CORES + c) for s, t in edge...  10.9 us
    pallas_call x3, Pallas kernels, alpha_product(): pl.pallas_call(body, in_specs=[pl.BlockSpec(memory_space=pltpu.VMEM)] * (...  8.47 us
    unnamed x25, local copies, waits for them, and re-layouts  5.88 us
    pallas_call x1, Pallas kernels, beta_product(): pl.pallas_call(body, grid_spec=pltpu.PrefetchScalarGridSpec(num_scalar_pr...  5.08 us
    all_to_all x1, starting transfers between devices, exchange(): lax.all_to_all(packed, 'beta', split_axis=0, concat_axis=0, tiled=True)  4.57 us
    ppermute x6, waiting for transfers between devices, swap(): lax.ppermute(x, 'alpha', [(p * CORES + c, p * CORES + 1 - c) for p in chi...  4.45 us
    slice x2, local copies, waits for them, and re-layouts, per_device(): coefficients[f * block:(f + n) * block]  3.06 us
  transfers between devices with their start and end apart: 12, of which 7 were waited for; matrix products, arithmetic and copies ran while one was open for 10% of the time, Pallas kernels for 20%

profile of v4, /device:TPU:0, one launch (start us, length us, event | category | flops | bytes accessed | tf_op | source)
XLA Modules:
  0.0 78.9 jit_solution(2374418879335074253)
XLA Ops:
  0.0 3.1 %collective-permute-start.4 = (bf16[512,1024]{1,0:T(8,128)(2,1)}, bf16[512,1024]{1,0:T(8,128)(2,1)}, u32[]{:S(2)}, u32[]{:S(2)}) collective-permute-start(bf16[512,1024]{1,0:T(8,128)(2,1)} %c_ref.2), channel_id=1, source_target_pairs={{0,8},{4,12},{8,0},{12,4},{16,24},{20,28},{24,16},{28,20},{1,9},{5... | collective-permute-start | bytes 3145736 | tf_op jit(solution)/shard_map/ppermute | solution.py:144
  3.1 1.0 %slice.12 = bf16[128,1024]{1,0:T(8,128)(2,1)S(1)} slice(bf16[512,1024]{1,0:T(8,128)(2,1)} %c_ref.2), slice={[0:128], [0:1024]} | slice | bytes 524288 | tf_op jit(solution)/shard_map/slice | solution.py:208
  4.1 2.7 %collective-permute-start = (bf16[128,1024]{1,0:T(8,128)(2,1)S(1)}, bf16[128,1024]{1,0:T(8,128)(2,1)S(1)}, u32[]{:S(2)}, u32[]{:S(2)}) collective-permute-start(bf16[128,1024]{1,0:T(8,128)(2,1)S(1)} %slice.12), channel_id=1, source_target_pairs={{0,16},{4,20},{8,24},{12,28},{16,0},{20,4},{24,8},{28,12},{1,17},{... | collective-permute-start | bytes 786440 | tf_op jit(solution)/shard_map/ppermute | solution.py:144
  6.8 2.1 %slice.13 = bf16[384,1024]{1,0:T(8,128)(2,1)} slice(bf16[512,1024]{1,0:T(8,128)(2,1)} %c_ref.2), slice={[128:512], [0:1024]} | slice | bytes 1572864 | tf_op jit(solution)/shard_map/slice | solution.py:208
  10.3 1.1 %pack_beta.1 = bf16[4,512,512]{2,1,0:T(8,128)(2,1)S(1)} custom-call(s32[16]{0:T(128)S(1)} %max.8.pack_ref, bf16[512,1024]{1,0:T(8,128)(2,1)S(1)} %copy-done.1), custom_call_target="tpu_custom_call" | custom-call | tf_op jit(solution)/shard_map/pack_beta/pallas_call | solution.py:51
  11.4 1.3 %copy-done.5 = bf16[4,512,512]{2,1,0:T(8,128)(2,1)} copy-done((bf16[4,512,512]{2,1,0:T(8,128)(2,1)}, bf16[4,512,512]{2,1,0:T(8,128)(2,1)S(1)}, u32[]{:S(2)}) %copy-start.5) | copy-done | bytes 2097176
  12.8 4.6 %all-to-all-start = ((bf16[4,512,512]{2,1,0:T(8,128)(2,1)}), bf16[4,512,512]{2,1,0:T(8,128)(2,1)}, u32[]{:S(2)}, u32[]{:S(2)}) async-start(bf16[4,512,512]{2,1,0:T(8,128)(2,1)} %copy-done.5), calls=%async_computation | async-start | bytes 4194304 | tf_op jit(solution)/shard_map/all_to_all | solution.py:189
  19.9 12.6 %collective-permute-done.rest_2_ = bf16[128,1024]{1,0:T(8,128)(2,1)S(1)} collective-permute-done((bf16[128,1024]{1,0:T(8,128)(2,1)S(1)}, bf16[128,1024]{1,0:T(8,128)(2,1)S(1)}, u32[]{:S(2)}, u32[]{:S(2)}) %collective-permute-start) | collective-permute-done | bytes 262176 | tf_op jit(solution)/shard_map/ppermute | solution.py:144
  32.5 3.5 %collective-permute-start.1 = (bf16[128,1024]{1,0:T(8,128)(2,1)S(1)}, bf16[128,1024]{1,0:T(8,128)(2,1)}, u32[]{:S(2)}, u32[]{:S(2)}) collective-permute-start(bf16[128,1024]{1,0:T(8,128)(2,1)S(1)} %collective-permute-done.rest_2_), channel_id=1, source_target_pairs={{0,8},{4,12},{8,0},{12,4},{16,24},{20,28},{24,16},{28,20},{1,9},{5... | collective-permute-start | bytes 786440 | tf_op jit(solution)/shard_map/ppermute | solution.py:144
  36.1 11.9 %collective-permute-done.4.rest_1_ = bf16[512,1024]{1,0:T(8,128)(2,1)} collective-permute-done((bf16[512,1024]{1,0:T(8,128)(2,1)}, bf16[512,1024]{1,0:T(8,128)(2,1)}, u32[]{:S(2)}, u32[]{:S(2)}) %collective-permute-start.4) | collective-permute-done | bytes 1048608 | tf_op jit(solution)/shard_map/ppermute | solution.py:144
  49.2 0.7 copy-done.8
  50.6 1.4 %lay_out.3.w_ref = bf16[512,3328]{1,0:T(8,128)(2,1)S(1)} custom-call(s32[104]{0:T(128)S(1)} %reshape.165.table_ref, bf16[4,14,128,128]{3,2,1,0:T(8,128)(2,1)S(1)} %copy-done.2), custom_call_target="tpu_custom_call" | custom-call | tf_op jit(solution)/shard_map/lay_out/pallas_call | solution.py:109
  52.0 1.7 %copy-done.3 = bf16[512,3328]{1,0:T(8,128)(2,1)} copy-done((bf16[512,3328]{1,0:T(8,128)(2,1)}, bf16[512,3328]{1,0:T(8,128)(2,1)S(1)}, u32[]{:S(2)}) %copy-start.3) | copy-done | bytes 3407896
  53.7 0.8 constant_dynamic-slice_fusion.4
  55.1 1.3 %collective-permute-start.3 = (bf16[384,1024]{1,0:T(8,128)(2,1)}, bf16[384,1024]{1,0:T(8,128)(2,1)S(1)}, u32[]{:S(2)}, u32[]{:S(2)}) collective-permute-start(bf16[384,1024]{1,0:T(8,128)(2,1)} %collective-permute-done.2.rest_3_), channel_id=1, source_target_pairs={{0,8},{4,12},{8,0},{12,4},{16,24},{20,28},{24,16},{28,20},{1,9},{5... | collective-permute-start | bytes 2359304 | tf_op jit(solution)/shard_map/ppermute | solution.py:144
  56.7 1.3 %collective-permute-done.7.rest_7_ = bf16[128,1024]{1,0:T(8,128)(2,1)S(1)} collective-permute-done((bf16[128,1024]{1,0:T(8,128)(2,1)S(1)}, bf16[128,1024]{1,0:T(8,128)(2,1)S(1)}, u32[]{:S(2)}, u32[]{:S(2)}) %collective-permute-start.7) | collective-permute-done | bytes 262176 | tf_op jit(solution)/shard_map/ppermute | solution.py:148
  58.3 1.6 %collective-permute-done.9.rest_9_ = bf16[128,1024]{1,0:T(8,128)(2,1)} collective-permute-done((bf16[128,1024]{1,0:T(8,128)(2,1)}, bf16[128,1024]{1,0:T(8,128)(2,1)}, u32[]{:S(2)}, u32[]{:S(2)}) %collective-permute-start.9) | collective-permute-done | bytes 262176 | tf_op jit(solution)/shard_map/ppermute | solution.py:148
  59.9 2.0 %copy-done.4 = bf16[512,3328]{1,0:T(8,128)(2,1)S(1)} copy-done((bf16[512,3328]{1,0:T(8,128)(2,1)S(1)}, bf16[512,3328]{1,0:T(8,128)(2,1)}, u32[]{:S(2)}) %copy-start.4) | copy-done | bytes 3407896
  61.9 6.1 %alpha_product.3.acc_ref = f32[512,1024]{1,0:T(8,128)S(1)} custom-call(bf16[512,3328]{1,0:T(8,128)(2,1)S(1)} %copy-done.4, bf16[512,1024]{1,0:T(8,128)(2,1)S(1)} %copy-done.1, bf16[512,1024]{1,0:T(8,128)(2,1)} %collective-permute-done.4.rest_1_, bf16[128,1024]{1,0:T(8,128)(2,1)S(1)} %collective-permute-done.rest_2_, ...), custom_call_target="tpu_custom_call" | custom-call | tf_op jit(solution)/shard_map/alpha_product/pallas_call | solution.py:133
  68.0 5.1 %beta_product.1.rest_0_ = f32[512,1024]{1,0:T(8,128)S(1)} custom-call(s32[128]{0:T(128)S(1)} %reshape.168.table_ref, bf16[8,14,128,128]{3,2,1,0:T(8,128)(2,1)S(1)} %copy-done.6, f32[512,1024]{1,0:T(8,128)S(1)} %copy-done.7, bf16[512,1024]{1,0:T(8,128)(2,1)S(1)} %copy-done.1, bf16[4,512,512]{2,1,0:T(8,128)(2,1)} %all-to-all-done.x_ref, ...), custom_call_target="tpu_custom_call" | custom-call | tf_op jit(solution)/shard_map/beta_product/pallas_call | solution.py:87
  73.1 1.8 %collective-permute-done.3.rest_1_ = bf16[384,1024]{1,0:T(8,128)(2,1)S(1)} collective-permute-done((bf16[384,1024]{1,0:T(8,128)(2,1)}, bf16[384,1024]{1,0:T(8,128)(2,1)S(1)}, u32[]{:S(2)}, u32[]{:S(2)}) %collective-permute-start.3) | collective-permute-done | bytes 786464 | tf_op jit(solution)/shard_map/ppermute | solution.py:144
  74.9 0.7 alpha_product.4.rest_0_
  75.6 1.6 %collective-permute-done.10.rest_1_ = bf16[384,1024]{1,0:T(8,128)(2,1)S(1)} collective-permute-done((bf16[384,1024]{1,0:T(8,128)(2,1)S(1)}, bf16[384,1024]{1,0:T(8,128)(2,1)S(1)}, u32[]{:S(2)}, u32[]{:S(2)}) %collective-permute-start.10) | collective-permute-done | bytes 786464 | tf_op jit(solution)/shard_map/ppermute | solution.py:148
  77.2 1.7 %alpha_product.5 = bf16[512,1024]{1,0:T(8,128)(2,1)} custom-call(bf16[512,384]{1,0:T(8,128)(2,1)S(1)} %lay_out.5.w_ref, f32[512,1024]{1,0:T(8,128)S(1)} %alpha_product.4.rest_0_, bf16[384,1024]{1,0:T(8,128)(2,1)S(1)} %collective-permute-done.10.rest_1_), custom_call_target="tpu_custom_call" | custom-call | tf_op jit(solution)/shard_map/alpha_product/pallas_call | solution.py:133
  (66 shorter events, 7.1 us)
Async XLA Ops:
  0.0 17.5 %copy-start = (s32[32,14]{0,1:T(8,128)S(1)}, s32[32,14]{0,1:T(8,128)}, u32[]{:S(2)}) copy-start(s32[32,14]{0,1:T(8,128)} %param.11) | copy-start | bytes 5380
  0.0 10.3 %copy-start.1 = (bf16[512,1024]{1,0:T(8,128)(2,1)S(1)}, bf16[512,1024]{1,0:T(8,128)(2,1)}, u32[]{:S(2)}) copy-start(bf16[512,1024]{1,0:T(8,128)(2,1)} %c_ref.2) | copy-start | bytes 3145732
  0.0 9.2 %copy-start.10 = (s32[32,14]{0,1:T(8,128)S(1)}, s32[32,14]{0,1:T(8,128)}, u32[]{:S(2)}) copy-start(s32[32,14]{0,1:T(8,128)} %param.13) | copy-start | bytes 5380
  0.0 48.0 %collective-permute-start.4 = (bf16[512,1024]{1,0:T(8,128)(2,1)}, bf16[512,1024]{1,0:T(8,128)(2,1)}, u32[]{:S(2)}, u32[]{:S(2)}) collective-permute-start(bf16[512,1024]{1,0:T(8,128)(2,1)} %c_ref.2), channel_id=1, source_target_pairs={{0,8},{4,12},{8,0},{12,4},{16,24},{20,28},{24,16},{28,20},{1,9},{5... | collective-permute-start | bytes 3145736 | tf_op jit(solution)/shard_map/ppermute | solution.py:144
  3.1 55.2 %collective-permute-start.5 = (bf16[512,1024]{1,0:T(8,128)(2,1)}, bf16[512,1024]{1,0:T(8,128)(2,1)}, u32[]{:S(2)}, u32[]{:S(2)}) collective-permute-start(bf16[512,1024]{1,0:T(8,128)(2,1)} %c_ref.2), channel_id=1, source_target_pairs={{0,4},{4,0},{8,12},{12,8},{16,20},{20,16},{24,28},{28,24},{1,5},{5... | collective-permute-start | bytes 3145736 | tf_op jit(solution)/shard_map/ppermute | solution.py:148
  4.1 28.4 %collective-permute-start = (bf16[128,1024]{1,0:T(8,128)(2,1)S(1)}, bf16[128,1024]{1,0:T(8,128)(2,1)S(1)}, u32[]{:S(2)}, u32[]{:S(2)}) collective-permute-start(bf16[128,1024]{1,0:T(8,128)(2,1)S(1)} %slice.12), channel_id=1, source_target_pairs={{0,16},{4,20},{8,24},{12,28},{16,0},{20,4},{24,8},{28,12},{1,17},{... | collective-permute-start | bytes 786440 | tf_op jit(solution)/shard_map/ppermute | solution.py:144
  8.8 45.8 %collective-permute-start.2 = (bf16[384,1024]{1,0:T(8,128)(2,1)}, bf16[384,1024]{1,0:T(8,128)(2,1)}, u32[]{:S(2)}, u32[]{:S(2)}) collective-permute-start(bf16[384,1024]{1,0:T(8,128)(2,1)} %slice.13), channel_id=1, source_target_pairs={{0,16},{4,20},{8,24},{12,28},{16,0},{20,4},{24,8},{28,12},{1,17},{... | collective-permute-start | bytes 2359304 | tf_op jit(solution)/shard_map/ppermute | solution.py:144
  11.4 1.4 %copy-start.5 = (bf16[4,512,512]{2,1,0:T(8,128)(2,1)}, bf16[4,512,512]{2,1,0:T(8,128)(2,1)S(1)}, u32[]{:S(2)}) copy-start(bf16[4,512,512]{2,1,0:T(8,128)(2,1)S(1)} %pack_beta.1) | copy-start | bytes 6291460
  12.8 35.7 %copy-start.2 = (bf16[4,14,128,128]{3,2,1,0:T(8,128)(2,1)S(1)}, bf16[4,14,128,128]{3,2,1,0:T(8,128)(2,1)}, u32[]{:S(2)}) copy-start(bf16[4,14,128,128]{3,2,1,0:T(8,128)(2,1)} %h_ref.6) | copy-start | bytes 5505028
  12.8 47.1 %all-to-all-start = ((bf16[4,512,512]{2,1,0:T(8,128)(2,1)}), bf16[4,512,512]{2,1,0:T(8,128)(2,1)}, u32[]{:S(2)}, u32[]{:S(2)}) async-start(bf16[4,512,512]{2,1,0:T(8,128)(2,1)} %copy-done.5), calls=%async_computation | async-start | bytes 4194304 | tf_op jit(solution)/shard_map/all_to_all | solution.py:189
  32.5 22.1 %collective-permute-start.1 = (bf16[128,1024]{1,0:T(8,128)(2,1)S(1)}, bf16[128,1024]{1,0:T(8,128)(2,1)}, u32[]{:S(2)}, u32[]{:S(2)}) collective-permute-start(bf16[128,1024]{1,0:T(8,128)(2,1)S(1)} %collective-permute-done.rest_2_), channel_id=1, source_target_pairs={{0,8},{4,12},{8,0},{12,4},{16,24},{20,28},{24,16},{28,20},{1,9},{5... | collective-permute-start | bytes 786440 | tf_op jit(solution)/shard_map/ppermute | solution.py:144
  48.0 11.9 %collective-permute-start.6 = (bf16[512,1024]{1,0:T(8,128)(2,1)}, bf16[512,1024]{1,0:T(8,128)(2,1)}, u32[]{:S(2)}, u32[]{:S(2)}) collective-permute-start(bf16[512,1024]{1,0:T(8,128)(2,1)} %collective-permute-done.4.rest_1_), channel_id=1, source_target_pairs={{0,4},{4,0},{8,12},{12,8},{16,20},{20,16},{24,28},{28,24},{1,5},{5... | collective-permute-start | bytes 3145736 | tf_op jit(solution)/shard_map/ppermute | solution.py:148
  49.2 0.7 copy-start.8
  50.6 3.9 %copy-start.11 = (s32[16]{0:T(128)S(1)}, s32[16]{0:T(128)}, u32[]{:S(2)}) copy-start(s32[16]{0:T(128)} %compare_select_fusion) | copy-start | bytes 196
  52.0 1.7 %copy-start.3 = (bf16[512,3328]{1,0:T(8,128)(2,1)}, bf16[512,3328]{1,0:T(8,128)(2,1)S(1)}, u32[]{:S(2)}) copy-start(bf16[512,3328]{1,0:T(8,128)(2,1)S(1)} %lay_out.3.w_ref) | copy-start | bytes 10223620
  54.7 5.2 %collective-permute-start.8 = (bf16[384,1024]{1,0:T(8,128)(2,1)}, bf16[384,1024]{1,0:T(8,128)(2,1)S(1)}, u32[]{:S(2)}, u32[]{:S(2)}) collective-permute-start(bf16[384,1024]{1,0:T(8,128)(2,1)} %collective-permute-done.2.rest_3_), channel_id=1, source_target_pairs={{0,4},{4,0},{8,12},{12,8},{16,20},{20,16},{24,28},{28,24},{1,5},{5... | collective-permute-start | bytes 2359304 | tf_op jit(solution)/shard_map/ppermute | solution.py:148
  55.1 19.7 %collective-permute-start.3 = (bf16[384,1024]{1,0:T(8,128)(2,1)}, bf16[384,1024]{1,0:T(8,128)(2,1)S(1)}, u32[]{:S(2)}, u32[]{:S(2)}) collective-permute-start(bf16[384,1024]{1,0:T(8,128)(2,1)} %collective-permute-done.2.rest_3_), channel_id=1, source_target_pairs={{0,8},{4,12},{8,0},{12,4},{16,24},{20,28},{24,16},{28,20},{1,9},{5... | collective-permute-start | bytes 2359304 | tf_op jit(solution)/shard_map/ppermute | solution.py:144
  56.5 1.5 %collective-permute-start.7 = (bf16[128,1024]{1,0:T(8,128)(2,1)S(1)}, bf16[128,1024]{1,0:T(8,128)(2,1)S(1)}, u32[]{:S(2)}, u32[]{:S(2)}) collective-permute-start(bf16[128,1024]{1,0:T(8,128)(2,1)S(1)} %collective-permute-done.rest_2_), channel_id=1, source_target_pairs={{0,4},{4,0},{8,12},{12,8},{16,20},{20,16},{24,28},{28,24},{1,5},{5... | collective-permute-start | bytes 786440 | tf_op jit(solution)/shard_map/ppermute | solution.py:148
  58.0 1.9 %collective-permute-start.9 = (bf16[128,1024]{1,0:T(8,128)(2,1)}, bf16[128,1024]{1,0:T(8,128)(2,1)}, u32[]{:S(2)}, u32[]{:S(2)}) collective-permute-start(bf16[128,1024]{1,0:T(8,128)(2,1)} %collective-permute-done.1.rest_4_), channel_id=1, source_target_pairs={{0,4},{4,0},{8,12},{12,8},{16,20},{20,16},{24,28},{28,24},{1,5},{5... | collective-permute-start | bytes 786440 | tf_op jit(solution)/shard_map/ppermute | solution.py:148
  59.9 2.0 %copy-start.4 = (bf16[512,3328]{1,0:T(8,128)(2,1)S(1)}, bf16[512,3328]{1,0:T(8,128)(2,1)}, u32[]{:S(2)}) copy-start(bf16[512,3328]{1,0:T(8,128)(2,1)} %copy-done.3) | copy-start | bytes 10223620
  61.9 6.1 %copy-start.6 = (bf16[8,14,128,128]{3,2,1,0:T(8,128)(2,1)S(1)}, bf16[8,14,128,128]{3,2,1,0:T(8,128)(2,1)}, u32[]{:S(2)}) copy-start(bf16[8,14,128,128]{3,2,1,0:T(8,128)(2,1)} %h_ref.7) | copy-start | bytes 11010052
  61.9 6.1 %copy-start.7 = (f32[512,1024]{1,0:T(8,128)S(1)}, f32[512,1024]{1,0:T(8,128)}, u32[]{:S(2)}) copy-start(f32[512,1024]{1,0:T(8,128)} %d_ref.1) | copy-start | bytes 6291460
  68.0 6.9 %copy-start.9 = (bf16[512,384]{1,0:T(8,128)(2,1)S(1)}, bf16[512,384]{1,0:T(8,128)(2,1)}, u32[]{:S(2)}) copy-start(bf16[512,384]{1,0:T(8,128)(2,1)} %copy-done.8) | copy-start | bytes 1179652
  74.9 2.3 %collective-permute-start.10 = (bf16[384,1024]{1,0:T(8,128)(2,1)S(1)}, bf16[384,1024]{1,0:T(8,128)(2,1)S(1)}, u32[]{:S(2)}, u32[]{:S(2)}) collective-permute-start(bf16[384,1024]{1,0:T(8,128)(2,1)S(1)} %collective-permute-done.3.rest_1_), channel_id=1, source_target_pairs={{0,4},{4,0},{8,12},{12,8},{16,20},{20,16},{24,28},{28,24},{1,5},{5... | collective-permute-start | bytes 2359304 | tf_op jit(solution)/shard_map/ppermute | solution.py:148

commit v5 on v4

--- a/solution.py
+++ b/solution.py
@@ -210,15 +210,15 @@
         near_far = send(far_own[0], near)
         own_swapped = swap(coefficients, everyone)
         arrived = exchange()
-        weights = [lay_out(table, alpha_blocks) for table in tables]
-        near_far, far_own[1], here, table_b, *weights = gate(near_far, far_own[1], coefficients, table_b, *weights)
+        near_far, far_own[1], here, table_b, *tables = gate(near_far, far_own[1], coefficients, table_b, *tables)
         near_last = send(far_own[1], near)
         pieces = [here, near_own, *far_own, near_far]
         pieces += [own_swapped] + [swap(x, everyone) for x in pieces[1:]]
-        *pieces, here, arrived = gate(*pieces, here, arrived)
+        *pieces, here, blocks_here, arrived = gate(*pieces, here, alpha_blocks, arrived)
+        weights = [lay_out(table, blocks_here) for table in tables]
         acc = alpha_product(weights[0], pieces, None, jnp.float32)
         acc = beta_product(table_b, beta_blocks, here, diagonal, arrived, acc)
-        near_last, acc = gate(near_last, acc)
+        near_last, acc, *weights = gate(near_last, acc, *weights)
         acc = alpha_product(weights[1], [near_last], acc, jnp.float32)
         return alpha_product(weights[2], [swap(near_last, everyone)], acc, jnp.bfloat16)
 

time: 79.3 us -> 79.5 us (level)
  local copies, waits for them, and re-layouts: 12.4 us -> 7.91 us
  waiting for transfers between devices: 30.9 us -> 34.8 us
  Pallas kernels: 17.3 us -> 18.5 us
    ppermute x5, waiting for transfers between devices: 26.4 us -> 31.9 us  [send(): lax.ppermute(x, 'alpha', [(s * CORES + c, t * CORES + c) for s, t in edge...]
    unnamed x25 -> x19, local copies, waits for them, and re-layouts: 5.88 us -> 2.12 us
    ppermute x6, waiting for transfers between devices: 4.45 us -> 2.88 us  [swap(): lax.ppermute(x, 'alpha', [(p * CORES + c, p * CORES + 1 - c) for p in chi...]
    pallas_call x3, Pallas kernels: 8.47 us -> 9.77 us  [alpha_product(): pl.pallas_call(body, in_specs=[pl.BlockSpec(memory_space=pltpu.VMEM)] * (...]
  transfers between devices with their start and end apart: 12 -> 12, of which waited for: 7 -> 7; matrix products, arithmetic and copies ran while one was open for 10% -> 9% of each run, Pallas kernels for 20% -> 21%
where the time goes in v5:
time: 79.5 us; the launch traced here: 79.1 us
  waiting for transfers between devices  34.8 us (44%)
  Pallas kernels  18.5 us (23%)
  starting transfers between devices  16.5 us (21%)
  local copies, waits for them, and re-layouts  7.91 us (10%)
  other arithmetic  1.15 us (1%)
    ppermute x5, waiting for transfers between devices, send(): lax.ppermute(x, 'alpha', [(s * CORES + c, t * CORES + c) for s, t in edge...  31.9 us
    ppermute x5, starting transfers between devices, send(): lax.ppermute(x, 'alpha', [(s * CORES + c, t * CORES + c) for s, t in edge...  11.4 us
    pallas_call x3, Pallas kernels, alpha_product(): pl.pallas_call(body, in_specs=[pl.BlockSpec(memory_space=pltpu.VMEM)] * (...  9.77 us
    pallas_call x1, Pallas kernels, beta_product(): pl.pallas_call(body, grid_spec=pltpu.PrefetchScalarGridSpec(num_scalar_pr...  5.02 us
    all_to_all x1, starting transfers between devices, exchange(): lax.all_to_all(packed, 'beta', split_axis=0, concat_axis=0, tiled=True)  4.57 us
    slice x2, local copies, waits for them, and re-layouts, per_device(): coefficients[f * block:(f + n) * block]  3.06 us
    ppermute x6, waiting for transfers between devices, swap(): lax.ppermute(x, 'alpha', [(p * CORES + c, p * CORES + 1 - c) for p in chi...  2.88 us
    pallas_call x3, Pallas kernels, lay_out(): pl.pallas_call(body, grid_spec=pltpu.PrefetchScalarGridSpec(num_scalar_pr...  2.65 us
  transfers between devices with their start and end apart: 12, of which 7 were waited for; matrix products, arithmetic and copies ran while one was open for 9% of the time, Pallas kernels for 21%

profile of v5, /device:TPU:0, one launch (start us, length us, event | category | flops | bytes accessed | tf_op | source)
XLA Modules:
  0.0 79.1 jit_solution(16636782660475092293)
XLA Ops:
  0.0 3.1 %collective-permute-start.4 = (bf16[512,1024]{1,0:T(8,128)(2,1)}, bf16[512,1024]{1,0:T(8,128)(2,1)}, u32[]{:S(2)}, u32[]{:S(2)}) collective-permute-start(bf16[512,1024]{1,0:T(8,128)(2,1)} %c_ref.2), channel_id=1, source_target_pairs={{0,8},{4,12},{8,0},{12,4},{16,24},{20,28},{24,16},{28,20},{1,9},{5... | collective-permute-start | bytes 3145736 | tf_op jit(solution)/shard_map/ppermute | solution.py:144
  3.1 1.0 %slice.12 = bf16[128,1024]{1,0:T(8,128)(2,1)S(1)} slice(bf16[512,1024]{1,0:T(8,128)(2,1)} %c_ref.2), slice={[0:128], [0:1024]} | slice | bytes 524288 | tf_op jit(solution)/shard_map/slice | solution.py:208
  4.1 2.7 %collective-permute-start = (bf16[128,1024]{1,0:T(8,128)(2,1)S(1)}, bf16[128,1024]{1,0:T(8,128)(2,1)S(1)}, u32[]{:S(2)}, u32[]{:S(2)}) collective-permute-start(bf16[128,1024]{1,0:T(8,128)(2,1)S(1)} %slice.12), channel_id=1, source_target_pairs={{0,16},{4,20},{8,24},{12,28},{16,0},{20,4},{24,8},{28,12},{1,17},{... | collective-permute-start | bytes 786440 | tf_op jit(solution)/shard_map/ppermute | solution.py:144
  6.8 2.1 %slice.13 = bf16[384,1024]{1,0:T(8,128)(2,1)} slice(bf16[512,1024]{1,0:T(8,128)(2,1)} %c_ref.2), slice={[128:512], [0:1024]} | slice | bytes 1572864 | tf_op jit(solution)/shard_map/slice | solution.py:208
  10.3 1.1 %pack_beta.1 = bf16[4,512,512]{2,1,0:T(8,128)(2,1)S(1)} custom-call(s32[16]{0:T(128)S(1)} %max.8.pack_ref, bf16[512,1024]{1,0:T(8,128)(2,1)S(1)} %copy-done.1), custom_call_target="tpu_custom_call" | custom-call | tf_op jit(solution)/shard_map/pack_beta/pallas_call | solution.py:51
  11.4 1.3 %copy-done.3 = bf16[4,512,512]{2,1,0:T(8,128)(2,1)} copy-done((bf16[4,512,512]{2,1,0:T(8,128)(2,1)}, bf16[4,512,512]{2,1,0:T(8,128)(2,1)S(1)}, u32[]{:S(2)}) %copy-start.3) | copy-done | bytes 2097176
  12.7 4.6 %all-to-all-start = ((bf16[4,512,512]{2,1,0:T(8,128)(2,1)}), bf16[4,512,512]{2,1,0:T(8,128)(2,1)}, u32[]{:S(2)}, u32[]{:S(2)}) async-start(bf16[4,512,512]{2,1,0:T(8,128)(2,1)} %copy-done.3), calls=%async_computation | async-start | bytes 4194304 | tf_op jit(solution)/shard_map/all_to_all | solution.py:189
  17.7 0.7 fusion.4
  18.4 0.7 fusion.3
  19.4 13.1 %collective-permute-done.rest_2_ = bf16[128,1024]{1,0:T(8,128)(2,1)S(1)} collective-permute-done((bf16[128,1024]{1,0:T(8,128)(2,1)S(1)}, bf16[128,1024]{1,0:T(8,128)(2,1)S(1)}, u32[]{:S(2)}, u32[]{:S(2)}) %collective-permute-start) | collective-permute-done | bytes 262176 | tf_op jit(solution)/shard_map/ppermute | solution.py:144
  32.5 3.5 %collective-permute-start.1 = (bf16[128,1024]{1,0:T(8,128)(2,1)S(1)}, bf16[128,1024]{1,0:T(8,128)(2,1)S(1)}, u32[]{:S(2)}, u32[]{:S(2)}) collective-permute-start(bf16[128,1024]{1,0:T(8,128)(2,1)S(1)} %collective-permute-done.rest_2_), channel_id=1, source_target_pairs={{0,8},{4,12},{8,0},{12,4},{16,24},{20,28},{24,16},{28,20},{1,9},{5... | collective-permute-start | bytes 786440 | tf_op jit(solution)/shard_map/ppermute | solution.py:144
  36.1 11.9 %collective-permute-done.4.rest_1_ = bf16[512,1024]{1,0:T(8,128)(2,1)} collective-permute-done((bf16[512,1024]{1,0:T(8,128)(2,1)}, bf16[512,1024]{1,0:T(8,128)(2,1)}, u32[]{:S(2)}, u32[]{:S(2)}) %collective-permute-start.4) | collective-permute-done | bytes 1048608 | tf_op jit(solution)/shard_map/ppermute | solution.py:144
  48.2 6.3 %collective-permute-done.1.rest_4_ = bf16[128,1024]{1,0:T(8,128)(2,1)S(1)} collective-permute-done((bf16[128,1024]{1,0:T(8,128)(2,1)S(1)}, bf16[128,1024]{1,0:T(8,128)(2,1)S(1)}, u32[]{:S(2)}, u32[]{:S(2)}) %collective-permute-start.1) | collective-permute-done | bytes 262176 | tf_op jit(solution)/shard_map/ppermute | solution.py:144
  54.6 1.8 %collective-permute-start.3 = (bf16[384,1024]{1,0:T(8,128)(2,1)}, bf16[384,1024]{1,0:T(8,128)(2,1)}, u32[]{:S(2)}, u32[]{:S(2)}) collective-permute-start(bf16[384,1024]{1,0:T(8,128)(2,1)} %collective-permute-done.2.rest_3_), channel_id=1, source_target_pairs={{0,8},{4,12},{8,0},{12,4},{16,24},{20,28},{24,16},{28,20},{1,9},{5... | collective-permute-start | bytes 2359304 | tf_op jit(solution)/shard_map/ppermute | solution.py:144
  56.6 1.3 %collective-permute-done.7.rest_7_ = bf16[128,1024]{1,0:T(8,128)(2,1)S(1)} collective-permute-done((bf16[128,1024]{1,0:T(8,128)(2,1)S(1)}, bf16[128,1024]{1,0:T(8,128)(2,1)S(1)}, u32[]{:S(2)}, u32[]{:S(2)}) %collective-permute-start.7) | collective-permute-done | bytes 262176 | tf_op jit(solution)/shard_map/ppermute | solution.py:148
  57.9 0.7 copy-done.6
  59.3 0.9 %collective-permute-done.9.rest_9_ = bf16[128,1024]{1,0:T(8,128)(2,1)} collective-permute-done((bf16[128,1024]{1,0:T(8,128)(2,1)S(1)}, bf16[128,1024]{1,0:T(8,128)(2,1)}, u32[]{:S(2)}, u32[]{:S(2)}) %collective-permute-start.9) | collective-permute-done | bytes 262176 | tf_op jit(solution)/shard_map/ppermute | solution.py:148
  60.3 1.4 %lay_out.3.w_ref = bf16[512,3328]{1,0:T(8,128)(2,1)S(1)} custom-call(s32[104]{0:T(128)S(1)} %reshape.166.table_ref, bf16[4,14,128,128]{3,2,1,0:T(8,128)(2,1)S(1)} %copy-done.2), custom_call_target="tpu_custom_call" | custom-call | tf_op jit(solution)/shard_map/lay_out/pallas_call | solution.py:109
  61.7 0.6 lay_out.4.w_ref
  63.0 6.3 %alpha_product.3.acc_ref = f32[512,1024]{1,0:T(8,128)S(1)} custom-call(bf16[512,3328]{1,0:T(8,128)(2,1)S(1)} %lay_out.3.w_ref, bf16[512,1024]{1,0:T(8,128)(2,1)S(1)} %copy-done.1, bf16[512,1024]{1,0:T(8,128)(2,1)} %collective-permute-done.4.rest_1_, bf16[128,1024]{1,0:T(8,128)(2,1)S(1)} %collective-permute-done.rest_2_, ...), custom_call_target="tpu_custom_call" | custom-call | tf_op jit(solution)/shard_map/alpha_product/pallas_call | solution.py:133
  69.3 5.0 %beta_product.1.rest_0_ = f32[512,1024]{1,0:T(8,128)S(1)} custom-call(s32[128]{0:T(128)S(1)} %reshape.165.table_ref, bf16[8,14,128,128]{3,2,1,0:T(8,128)(2,1)S(1)} %copy-done.4, f32[512,1024]{1,0:T(8,128)S(1)} %copy-done.5, bf16[512,1024]{1,0:T(8,128)(2,1)S(1)} %copy-done.1, bf16[4,512,512]{2,1,0:T(8,128)(2,1)} %all-to-all-done.x_ref, ...), custom_call_target="tpu_custom_call" | custom-call | tf_op jit(solution)/shard_map/beta_product/pallas_call | solution.py:87
  74.9 1.8 %alpha_product.4.rest_0_ = f32[512,1024]{1,0:T(8,128)S(1)} custom-call(bf16[512,384]{1,0:T(8,128)(2,1)S(1)} %lay_out.4.w_ref, f32[512,1024]{1,0:T(8,128)S(1)} %beta_product.1.rest_0_, bf16[384,1024]{1,0:T(8,128)(2,1)} %collective-permute-done.3.rest_1_), custom_call_target="tpu_custom_call" | custom-call | tf_op jit(solution)/shard_map/alpha_product/pallas_call | solution.py:133
  76.7 0.6 collective-permute-done.10.rest_1_
  77.4 1.7 %alpha_product.5 = bf16[512,1024]{1,0:T(8,128)(2,1)} custom-call(bf16[512,384]{1,0:T(8,128)(2,1)S(1)} %lay_out.5.w_ref, f32[512,1024]{1,0:T(8,128)S(1)} %alpha_product.4.rest_0_, bf16[384,1024]{1,0:T(8,128)(2,1)S(1)} %collective-permute-done.10.rest_1_), custom_call_target="tpu_custom_call" | custom-call | tf_op jit(solution)/shard_map/alpha_product/pallas_call | solution.py:133
  (60 shorter events, 4.6 us)
Async XLA Ops:
  0.0 17.6 %copy-start = (s32[32,14]{0,1:T(8,128)S(1)}, s32[32,14]{0,1:T(8,128)}, u32[]{:S(2)}) copy-start(s32[32,14]{0,1:T(8,128)} %param.11) | copy-start | bytes 5380
  0.0 10.3 %copy-start.1 = (bf16[512,1024]{1,0:T(8,128)(2,1)S(1)}, bf16[512,1024]{1,0:T(8,128)(2,1)}, u32[]{:S(2)}) copy-start(bf16[512,1024]{1,0:T(8,128)(2,1)} %c_ref.2) | copy-start | bytes 3145732
  0.0 9.2 %copy-start.8 = (s32[32,14]{0,1:T(8,128)S(1)}, s32[32,14]{0,1:T(8,128)}, u32[]{:S(2)}) copy-start(s32[32,14]{0,1:T(8,128)} %param.13) | copy-start | bytes 5380
  0.0 48.0 %collective-permute-start.4 = (bf16[512,1024]{1,0:T(8,128)(2,1)}, bf16[512,1024]{1,0:T(8,128)(2,1)}, u32[]{:S(2)}, u32[]{:S(2)}) collective-permute-start(bf16[512,1024]{1,0:T(8,128)(2,1)} %c_ref.2), channel_id=1, source_target_pairs={{0,8},{4,12},{8,0},{12,4},{16,24},{20,28},{24,16},{28,20},{1,9},{5... | collective-permute-start | bytes 3145736 | tf_op jit(solution)/shard_map/ppermute | solution.py:144
  3.1 57.2 %collective-permute-start.5 = (bf16[512,1024]{1,0:T(8,128)(2,1)}, bf16[512,1024]{1,0:T(8,128)(2,1)}, u32[]{:S(2)}, u32[]{:S(2)}) collective-permute-start(bf16[512,1024]{1,0:T(8,128)(2,1)} %c_ref.2), channel_id=1, source_target_pairs={{0,4},{4,0},{8,12},{12,8},{16,20},{20,16},{24,28},{28,24},{1,5},{5... | collective-permute-start | bytes 3145736 | tf_op jit(solution)/shard_map/ppermute | solution.py:148
  4.1 28.4 %collective-permute-start = (bf16[128,1024]{1,0:T(8,128)(2,1)S(1)}, bf16[128,1024]{1,0:T(8,128)(2,1)S(1)}, u32[]{:S(2)}, u32[]{:S(2)}) collective-permute-start(bf16[128,1024]{1,0:T(8,128)(2,1)S(1)} %slice.12), channel_id=1, source_target_pairs={{0,16},{4,20},{8,24},{12,28},{16,0},{20,4},{24,8},{28,12},{1,17},{... | collective-permute-start | bytes 786440 | tf_op jit(solution)/shard_map/ppermute | solution.py:144
  8.8 45.7 %collective-permute-start.2 = (bf16[384,1024]{1,0:T(8,128)(2,1)}, bf16[384,1024]{1,0:T(8,128)(2,1)}, u32[]{:S(2)}, u32[]{:S(2)}) collective-permute-start(bf16[384,1024]{1,0:T(8,128)(2,1)} %slice.13), channel_id=1, source_target_pairs={{0,16},{4,20},{8,24},{12,28},{16,0},{20,4},{24,8},{28,12},{1,17},{... | collective-permute-start | bytes 2359304 | tf_op jit(solution)/shard_map/ppermute | solution.py:144
  11.4 1.3 %copy-start.3 = (bf16[4,512,512]{2,1,0:T(8,128)(2,1)}, bf16[4,512,512]{2,1,0:T(8,128)(2,1)S(1)}, u32[]{:S(2)}) copy-start(bf16[4,512,512]{2,1,0:T(8,128)(2,1)S(1)} %pack_beta.1) | copy-start | bytes 6291460
  12.7 47.6 %copy-start.2 = (bf16[4,14,128,128]{3,2,1,0:T(8,128)(2,1)S(1)}, bf16[4,14,128,128]{3,2,1,0:T(8,128)(2,1)}, u32[]{:S(2)}) copy-start(bf16[4,14,128,128]{3,2,1,0:T(8,128)(2,1)} %h_ref.4) | copy-start | bytes 5505028
  12.7 47.5 %all-to-all-start = ((bf16[4,512,512]{2,1,0:T(8,128)(2,1)}), bf16[4,512,512]{2,1,0:T(8,128)(2,1)}, u32[]{:S(2)}, u32[]{:S(2)}) async-start(bf16[4,512,512]{2,1,0:T(8,128)(2,1)} %copy-done.3), calls=%async_computation | async-start | bytes 4194304 | tf_op jit(solution)/shard_map/all_to_all | solution.py:189
  32.5 22.0 %collective-permute-start.1 = (bf16[128,1024]{1,0:T(8,128)(2,1)S(1)}, bf16[128,1024]{1,0:T(8,128)(2,1)S(1)}, u32[]{:S(2)}, u32[]{:S(2)}) collective-permute-start(bf16[128,1024]{1,0:T(8,128)(2,1)S(1)} %collective-permute-done.rest_2_), channel_id=1, source_target_pairs={{0,8},{4,12},{8,0},{12,4},{16,24},{20,28},{24,16},{28,20},{1,9},{5... | collective-permute-start | bytes 786440 | tf_op jit(solution)/shard_map/ppermute | solution.py:144
  48.0 12.3 %collective-permute-start.6 = (bf16[512,1024]{1,0:T(8,128)(2,1)}, bf16[512,1024]{1,0:T(8,128)(2,1)}, u32[]{:S(2)}, u32[]{:S(2)}) collective-permute-start(bf16[512,1024]{1,0:T(8,128)(2,1)} %collective-permute-done.4.rest_1_), channel_id=1, source_target_pairs={{0,4},{4,0},{8,12},{12,8},{16,20},{20,16},{24,28},{28,24},{1,5},{5... | collective-permute-start | bytes 3145736 | tf_op jit(solution)/shard_map/ppermute | solution.py:148
  54.6 5.7 %collective-permute-start.8 = (bf16[384,1024]{1,0:T(8,128)(2,1)}, bf16[384,1024]{1,0:T(8,128)(2,1)}, u32[]{:S(2)}, u32[]{:S(2)}) collective-permute-start(bf16[384,1024]{1,0:T(8,128)(2,1)} %collective-permute-done.2.rest_3_), channel_id=1, source_target_pairs={{0,4},{4,0},{8,12},{12,8},{16,20},{20,16},{24,28},{28,24},{1,5},{5... | collective-permute-start | bytes 2359304 | tf_op jit(solution)/shard_map/ppermute | solution.py:148
  54.6 20.3 %collective-permute-start.3 = (bf16[384,1024]{1,0:T(8,128)(2,1)}, bf16[384,1024]{1,0:T(8,128)(2,1)}, u32[]{:S(2)}, u32[]{:S(2)}) collective-permute-start(bf16[384,1024]{1,0:T(8,128)(2,1)} %collective-permute-done.2.rest_3_), channel_id=1, source_target_pairs={{0,8},{4,12},{8,0},{12,4},{16,24},{20,28},{24,16},{28,20},{1,9},{5... | collective-permute-start | bytes 2359304 | tf_op jit(solution)/shard_map/ppermute | solution.py:144
  56.4 1.5 %collective-permute-start.7 = (bf16[128,1024]{1,0:T(8,128)(2,1)S(1)}, bf16[128,1024]{1,0:T(8,128)(2,1)S(1)}, u32[]{:S(2)}, u32[]{:S(2)}) collective-permute-start(bf16[128,1024]{1,0:T(8,128)(2,1)S(1)} %collective-permute-done.rest_2_), channel_id=1, source_target_pairs={{0,4},{4,0},{8,12},{12,8},{16,20},{20,16},{24,28},{28,24},{1,5},{5... | collective-permute-start | bytes 786440 | tf_op jit(solution)/shard_map/ppermute | solution.py:148
  57.9 0.7 copy-start.6
  58.6 1.7 %collective-permute-start.9 = (bf16[128,1024]{1,0:T(8,128)(2,1)S(1)}, bf16[128,1024]{1,0:T(8,128)(2,1)}, u32[]{:S(2)}, u32[]{:S(2)}) collective-permute-start(bf16[128,1024]{1,0:T(8,128)(2,1)S(1)} %collective-permute-done.1.rest_4_), channel_id=1, source_target_pairs={{0,4},{4,0},{8,12},{12,8},{16,20},{20,16},{24,28},{28,24},{1,5},{5... | collective-permute-start | bytes 786440 | tf_op jit(solution)/shard_map/ppermute | solution.py:148
  61.7 1.3 %copy-start.7 = (bf16[128,1024]{1,0:T(8,128)(2,1)S(1)}, bf16[128,1024]{1,0:T(8,128)(2,1)}, u32[]{:S(2)}) copy-start(bf16[128,1024]{1,0:T(8,128)(2,1)} %copy-done.6) | copy-start | bytes 786436
  63.0 6.3 %copy-start.4 = (bf16[8,14,128,128]{3,2,1,0:T(8,128)(2,1)S(1)}, bf16[8,14,128,128]{3,2,1,0:T(8,128)(2,1)}, u32[]{:S(2)}) copy-start(bf16[8,14,128,128]{3,2,1,0:T(8,128)(2,1)} %h_ref.2) | copy-start | bytes 11010052
  63.0 6.3 %copy-start.5 = (f32[512,1024]{1,0:T(8,128)S(1)}, f32[512,1024]{1,0:T(8,128)}, u32[]{:S(2)}) copy-start(f32[512,1024]{1,0:T(8,128)} %d_ref.1) | copy-start | bytes 6291460
  74.9 2.5 %collective-permute-start.10 = (bf16[384,1024]{1,0:T(8,128)(2,1)}, bf16[384,1024]{1,0:T(8,128)(2,1)S(1)}, u32[]{:S(2)}, u32[]{:S(2)}) collective-permute-start(bf16[384,1024]{1,0:T(8,128)(2,1)} %collective-permute-done.3.rest_1_), channel_id=1, source_target_pairs={{0,4},{4,0},{8,12},{12,8},{16,20},{20,16},{24,28},{28,24},{1,5},{5... | collective-permute-start | bytes 2359304 | tf_op jit(solution)/shard_map/ppermute | solution.py:148
